TPU v7x, 32 devices: a whole 2x2x4 slice. The times are simulated.
32 devices in a mesh: ba: 2 (over core), row: 4 (over y, x), col: 4 (over z).
Axes of the slice: x: 2, y: 2, z: 4, core: 2. Of those that a mesh axis runs over, the one named last changes fastest.
Arguments:
- tokens: bfloat16 [12288, 768], P(('ba', 'row', 'col')), may hold values from -6 to 6
- lengths: int32 [8, 4], P(('ba', 'row')), may hold values from 1 to 768, 1536 in all within a row
- w_query: bfloat16 [768, 768], P('row', 'col'), may hold values from -0.21875 to 0.21875
- w_key: bfloat16 [768, 768], P('row', 'col'), may hold values from -0.21875 to 0.21875
- w_value: bfloat16 [768, 768], P('row', 'col'), may hold values from -0.21875 to 0.21875
- w_out: bfloat16 [768, 768], P('col', 'row'), may hold values from -1.75 to 1.75
- w_gate: bfloat16 [768, 2048], P('row', 'col'), may hold values from -0.21875 to 0.21875
- w_up: bfloat16 [768, 2048], P('row', 'col'), may hold values from -0.21875 to 0.21875
- w_down: bfloat16 [2048, 768], P('col', 'row'), may hold values from -0.25 to 0.25
- gain_attn: float32 [768], replicated, may hold values from 0.5 to 1.5
- gain_mlp: float32 [768], replicated, may hold values from 0.5 to 1.5
- cotangent: bfloat16 [12288, 768], P(('ba', 'row', 'col')), may hold values from -6 to 6
Outputs:
- layer_out: bfloat16 [12288, 768], P(('ba', 'row', 'col'))
- input_grad: bfloat16 [12288, 768], P(('ba', 'row', 'col'))
- grad_query: float32 [768, 768], P('row', 'col')
- grad_key: float32 [768, 768], P('row', 'col')
- grad_value: float32 [768, 768], P('row', 'col')
- grad_out: float32 [768, 768], P('col', 'row')
- grad_gate: float32 [768, 2048], P('row', 'col')
- grad_up: float32 [768, 2048], P('row', 'col')
- grad_down: float32 [2048, 768], P('col', 'row')
- grad_gain_attn: float32 [768], replicated
- grad_gain_mlp: float32 [768], replicated
Inputs may be any that keep to these rules, and one draw needn't show every extreme that they name: `lengths`: each row sums to 1536, and its largest length is exactly 768.
All inputs are finite; a program needn't handle non-finite values.
Results may differ from a plain program's by a relative error of at most 0.015.
Values may be sent and summed in bfloat16 or wider, within the bound.
No kernel may reach another device: no remote copies, remote signals or barrier semaphores. Data moves between devices by JAX's collectives and lax.ppermute only.
A program may use at most 128 MiB of HBM per device.

v0:
```python
import jax
import jax.numpy as jnp
from jax import lax
from jax.sharding import PartitionSpec as P

D = 768
HEAD_DIM = 64


EPSILON = 1e-06
ROPE_BASE = 10000.0


def contract(left, right, first, second):
    return lax.dot_general(
        left, right, (((first,), (second,)), ((), ())), preferred_element_type=jnp.float32
    )


def locate(lengths, row_count):
    seq_count = lengths.shape[0]
    seq_ends = jnp.cumsum(lengths, dtype=jnp.int32)
    starts = seq_ends - lengths
    index = jnp.arange(row_count, dtype=jnp.int32)
    segment = jnp.sum(
        (index[:, None] >= seq_ends[None, :]).astype(jnp.int32), axis=1, dtype=jnp.int32
    )
    chosen = segment[:, None] == jnp.arange(seq_count, dtype=jnp.int32)[None, :]
    seq_start = jnp.sum(jnp.where(chosen, starts[None, :], 0), axis=1, dtype=jnp.int32)
    return (segment, index, index - seq_start)


def rotate(values, positions, direction):
    half_dim = values.shape[-1] // 2
    frequency = ROPE_BASE ** (-jnp.arange(half_dim, dtype=jnp.float32) / half_dim)
    angles = positions.astype(jnp.float32)[:, None] * frequency[None, :]
    cosine = jnp.cos(angles)[:, None, :]
    sine_part = jnp.sin(angles)[:, None, :]
    front_half = values[..., :half_dim]
    second = values[..., half_dim:]
    return jnp.concatenate(
        [
            front_half * cosine - direction * second * sine_part,
            second * cosine + direction * front_half * sine_part,
        ],
        axis=-1,
    )


def spread_normed(values):
    return lax.all_gather(values, "col", axis=0, tiled=True)


def again_normed(values):
    return lax.all_gather(values, "col", axis=0, tiled=True)


def spread_grads(values):
    return lax.all_gather(values, "col", axis=0, tiled=True)


def rows_in(values):
    return lax.psum_scatter(values, "row", scatter_dimension=0, tiled=True)


def rows_out(values):
    return lax.psum_scatter(values, "row", scatter_dimension=1, tiled=True)


def reduce_cols(block_rows, weight_local, flipped):
    return lax.psum_scatter(
        contract(block_rows, weight_local, 1, 1 if flipped else 0),
        "col",
        scatter_dimension=0,
        tiled=True,
    )


def norm_forward(values, gain_vec):
    row_scale = lax.rsqrt(jnp.mean(values * values, axis=1) + EPSILON)
    return (row_scale, values * row_scale[:, None] * gain_vec[None, :])


def norm_backward(values, row_scale, gain_vec, grad_normed):
    weighted = grad_normed * gain_vec[None, :]
    inner_sum = jnp.sum(weighted * values, axis=1)
    grad_values = row_scale[:, None] * weighted - values * (row_scale**3 * inner_sum / D)[:, None]
    gain_part = jnp.sum(grad_normed * values * row_scale[:, None], axis=0)
    return (grad_values, gain_part)


def attention_forward(query_rot, key_rot, value_low, segment, index):
    row_count = query_rot.shape[0]
    block_rows = min(512, row_count)
    blocks = row_count // block_rows

    def one_block(inputs):
        query_block, segment_block, index_block = inputs
        raw_scores = jnp.einsum(
            "qhd,khd->hqk", query_block, key_rot, preferred_element_type=jnp.float32
        )
        allowed = (segment_block[:, None] == segment[None, :]) & (
            index_block[:, None] >= index[None, :]
        )
        scores = jnp.where(allowed[None], raw_scores * HEAD_DIM ** (-0.5), -1e30)
        row_peak = jnp.max(scores, axis=-1)
        weights = jnp.exp(scores - row_peak[..., None])
        weight_sum = jnp.sum(weights, axis=-1)
        probabilities = (weights / weight_sum[..., None]).astype(jnp.bfloat16)
        head_out = jnp.einsum(
            "hqk,khd->qhd", probabilities, value_low, preferred_element_type=jnp.float32
        )
        return (head_out, row_peak + jnp.log(weight_sum))

    head_out, log_total = lax.map(
        one_block,
        (
            query_rot.reshape(blocks, block_rows, query_rot.shape[1], query_rot.shape[2]),
            segment.reshape(blocks, block_rows),
            index.reshape(blocks, block_rows),
        ),
    )
    return (head_out.reshape(query_rot.shape), log_total)


def attention_backward(query_rot, key_rot, value_low, grad_heads, log_total, segment, index):
    row_count = query_rot.shape[0]
    block_rows = min(512, row_count)
    blocks = row_count // block_rows
    block_shape = (blocks, block_rows, query_rot.shape[1], query_rot.shape[2])

    def one_block(grad_pair, inputs):
        grad_key_sum, grad_value_sum = grad_pair
        query_block, grad_block, log_block, segment_block, index_block = inputs
        raw_scores = jnp.einsum(
            "qhd,khd->hqk", query_block, key_rot, preferred_element_type=jnp.float32
        )
        allowed = (segment_block[:, None] == segment[None, :]) & (
            index_block[:, None] >= index[None, :]
        )
        scores = jnp.where(allowed[None], raw_scores * HEAD_DIM ** (-0.5), -1e30)
        probabilities = jnp.exp(scores - log_block[..., None])
        grad_probs = jnp.einsum(
            "qhd,khd->hqk", grad_block, value_low, preferred_element_type=jnp.float32
        )
        inner_sum = jnp.sum(probabilities * grad_probs, axis=-1, keepdims=True)
        grad_raw = (probabilities * (grad_probs - inner_sum) * HEAD_DIM ** (-0.5)).astype(
            jnp.bfloat16
        )
        grad_query = jnp.einsum(
            "hqk,khd->qhd", grad_raw, key_rot, preferred_element_type=jnp.float32
        )
        grad_key_sum = grad_key_sum + jnp.einsum(
            "hqk,qhd->khd", grad_raw, query_block, preferred_element_type=jnp.float32
        )
        grad_value_sum = grad_value_sum + jnp.einsum(
            "hqk,qhd->khd",
            probabilities.astype(jnp.bfloat16),
            grad_block,
            preferred_element_type=jnp.float32,
        )
        return ((grad_key_sum, grad_value_sum), grad_query)

    zero_grad = jnp.zeros(key_rot.shape, jnp.float32)
    (grad_key_sum, grad_value_sum), grad_query = lax.scan(
        one_block,
        (zero_grad, zero_grad),
        (
            query_rot.reshape(block_shape),
            grad_heads.reshape(block_shape),
            log_total,
            segment.reshape(blocks, block_rows),
            index.reshape(blocks, block_rows),
        ),
    )
    return (grad_query.reshape(query_rot.shape), grad_key_sum, grad_value_sum)


def shards(
    tokens,
    lengths,
    w_query,
    w_key,
    w_value,
    w_out,
    w_gate,
    w_up,
    w_down,
    gain_attn,
    gain_mlp,
    cotangent,
):
    col_count = w_query.shape[1]
    hidden_cols = w_gate.shape[1]
    heads_here = col_count // HEAD_DIM
    w_qkv = jnp.concatenate([w_query, w_key, w_value], axis=1)
    w_gate_up = jnp.concatenate([w_gate, w_up], axis=1)
    qkv_rows, gate_up_rows = (
        lax.all_gather(w_qkv, "row", axis=0, tiled=True),
        lax.all_gather(w_gate_up, "row", axis=0, tiled=True),
    )
    out_rows, down_rows = (
        lax.all_gather(w_out, "row", axis=1, tiled=True),
        lax.all_gather(w_down, "row", axis=1, tiled=True),
    )
    residual = tokens.astype(jnp.float32)
    scale_attn, normed = norm_forward(residual, gain_attn)
    normed_low = normed.astype(jnp.bfloat16)
    normed_all = spread_normed(normed_low)
    qkv_sums = contract(normed_all, qkv_rows, 1, 0)
    row_count = qkv_sums.shape[0]
    segment, index, positions = locate(lengths[0], row_count)
    head_shape = (row_count, heads_here, HEAD_DIM)
    query_rot = rotate(qkv_sums[:, :col_count].reshape(head_shape), positions, 1.0).astype(
        jnp.bfloat16
    )
    key_rot = rotate(
        qkv_sums[:, col_count : 2 * col_count].reshape(head_shape), positions, 1.0
    ).astype(jnp.bfloat16)
    value_low = qkv_sums[:, 2 * col_count :].reshape(head_shape).astype(jnp.bfloat16)
    head_values, log_total = attention_forward(query_rot, key_rot, value_low, segment, index)
    head_low = head_values.reshape(row_count, col_count).astype(jnp.bfloat16)
    middle = residual + reduce_cols(head_low, out_rows, False)
    scale_mlp, normed_mlp = norm_forward(middle, gain_mlp)
    normed_mlp_low = normed_mlp.astype(jnp.bfloat16)
    normed_mlp_all = spread_normed(normed_mlp_low)
    gate_up = contract(normed_mlp_all, gate_up_rows, 1, 0)
    gate_act = gate_up[:, :hidden_cols]
    up_act = gate_up[:, hidden_cols:]
    sigmoid_gate = jax.nn.sigmoid(gate_act)
    silu_gate = gate_act * sigmoid_gate
    hidden_low = (silu_gate * up_act).astype(jnp.bfloat16)
    layer_out = (middle + reduce_cols(hidden_low, down_rows, False)).astype(jnp.bfloat16)
    normed_mlp_back = again_normed(normed_mlp_low)
    grad_all = spread_grads(cotangent)
    grad_down = rows_out(contract(hidden_low, grad_all, 0, 0))
    grad_hidden = contract(grad_all, down_rows, 1, 1)
    grad_gate_act = grad_hidden * up_act * (sigmoid_gate + silu_gate * (1.0 - sigmoid_gate))
    grad_up_act = grad_hidden * silu_gate
    grad_gate_up = jnp.concatenate([grad_gate_act, grad_up_act], axis=1).astype(jnp.bfloat16)
    grad_gate_up_w = rows_in(contract(normed_mlp_back, grad_gate_up, 0, 0))
    grad_gate = grad_gate_up_w[:, :hidden_cols]
    grad_up = grad_gate_up_w[:, hidden_cols:]
    grad_normed_mlp = reduce_cols(grad_gate_up, gate_up_rows, True)
    grad_middle_norm, gain_mlp_part = norm_backward(middle, scale_mlp, gain_mlp, grad_normed_mlp)
    grad_middle = cotangent.astype(jnp.float32) + grad_middle_norm
    normed_back = again_normed(normed_low)
    grad_middle_low = grad_middle.astype(jnp.bfloat16)
    grad_middle_all = spread_grads(grad_middle_low)
    grad_out = rows_out(contract(head_low, grad_middle_all, 0, 0))
    grad_heads = contract(grad_middle_all, out_rows, 1, 1).reshape(head_shape).astype(jnp.bfloat16)
    grad_query_rot, grad_key_rot, grad_value_act = attention_backward(
        query_rot, key_rot, value_low, grad_heads, log_total, segment, index
    )
    grad_query_act = rotate(grad_query_rot, positions, -1.0)
    grad_key_act = rotate(grad_key_rot, positions, -1.0)
    grad_qkv = jnp.concatenate(
        [
            grad_query_act.reshape(row_count, col_count),
            grad_key_act.reshape(row_count, col_count),
            grad_value_act.reshape(row_count, col_count),
        ],
        axis=1,
    ).astype(jnp.bfloat16)
    grad_qkv_w = rows_in(contract(normed_back, grad_qkv, 0, 0))
    grad_normed = reduce_cols(grad_qkv, qkv_rows, True)
    grad_input_norm, gain_attn_part = norm_backward(residual, scale_attn, gain_attn, grad_normed)
    input_grad = (grad_middle + grad_input_norm).astype(jnp.bfloat16)
    grad_query = grad_qkv_w[:, :col_count]
    grad_key = grad_qkv_w[:, col_count : 2 * col_count]
    grad_value = grad_qkv_w[:, 2 * col_count :]
    grad_query, grad_key, grad_value, grad_out, grad_gate, grad_up, grad_down = lax.psum(
        (grad_query, grad_key, grad_value, grad_out, grad_gate, grad_up, grad_down), "ba"
    )
    grad_gain_attn, grad_gain_mlp = lax.psum((gain_attn_part, gain_mlp_part), ("ba", "row", "col"))
    return (
        layer_out,
        input_grad,
        grad_query,
        grad_key,
        grad_value,
        grad_out,
        grad_gate,
        grad_up,
        grad_down,
        grad_gain_attn,
        grad_gain_mlp,
    )


def solution(mesh):
    in_specs = (
        P(("ba", "row", "col"), None),
        P(("ba", "row"), None),
        P("row", "col"),
        P("row", "col"),
        P("row", "col"),
        P("col", "row"),
        P("row", "col"),
        P("row", "col"),
        P("col", "row"),
        P(),
        P(),
        P(("ba", "row", "col"), None),
    )
    out_specs = (
        P(("ba", "row", "col"), None),
        P(("ba", "row", "col"), None),
        P("row", "col"),
        P("row", "col"),
        P("row", "col"),
        P("col", "row"),
        P("row", "col"),
        P("row", "col"),
        P("col", "row"),
        P(),
        P(),
    )
    return jax.shard_map(shards, mesh=mesh, in_specs=in_specs, out_specs=out_specs, check_vma=False)
```

profile of v0, /device:TPU:0, one launch (start us, length us, event | category | flops | bytes accessed | tf_op | source)
XLA Modules:
  0.0 920.5 jit_solution(14454263457257708733)
XLA Ops:
  12.1 11.0 %all_gather.28 = bf16[192,768]{0,1:T(8,128)(2,1)S(1)} all-gather(bf16[192,192]{0,1:T(8,128)(2,1)S(1)} %copy.39), channel_id=1, replica_groups=mesh['ba'=2,'row'=4,'col'=4] {'row'}, dimensions={1}, use_global_device_ids=true | all-gather | bytes 368640 | tf_op jit(solution)/shard_map/all_gather | solution.py:203
  23.9 13.2 %all_gather.27 = bf16[768,576]{1,0:T(8,128)(2,1)S(1)} all-gather(bf16[192,576]{1,0:T(8,128)(2,1)S(1)} %pad_maximum_fusion.11), channel_id=1, replica_groups=mesh['ba'=2,'row'=4,'col'=4] {'row'}, dimensions={0}, use_global_device_ids=true | all-gather | bytes 1105920 | tf_op jit(solution)/shard_map/all_gather | solution.py:199
  38.6 26.4 %all-gather.6.cloned.1.call-done = bf16[1536,768]{1,0:T(8,128)(2,1)} async-done(((bf16[384,768]{1,0:T(8,128)(2,1)}), bf16[1536,768]{1,0:T(8,128)(2,1)}) %all-gather.6.cloned.1.call-update) | async-done | bytes 2359312 | tf_op jit(solution)/shard_map/all_gather | solution.py:51
  74.4 33.8 %while.28 = (s32[]{:T(128)}, bf16[3,512,3,64]{1,3,2,0:T(8,128)(2,1)}, f32[3,3,512]{2,1,0:T(4,128)S(1)}, s32[3,512]{1,0:T(4,128)S(1)}, s32[1536]{0:T(1024)S(1)}, ...) while((s32[]{:T(128)}, ...), condition=%wide.region_7.8_spmd.clone, body=%wide.region_4.7_spmd.clone.sunk | while | flops 634649088 | bytes 38023348 | solution.py:115
  114.9 82.4 %reduce-scatter.11.cloned.1.call-done = f32[384,768]{1,0:T(8,128)} async-done(((f32[1536,768]{1,0:T(8,128)}), f32[384,768]{1,0:T(8,128)}) %reduce-scatter.11.cloned.1.call-update) | async-done | bytes 1179664 | tf_op jit(solution)/shard_map/reduce_scatter | solution.py:71
  200.4 11.2 %all_gather.31 = bf16[512,768]{0,1:T(8,128)(2,1)S(1)} all-gather(bf16[512,192]{0,1:T(8,128)(2,1)S(1)} %copy-done.27), channel_id=1, replica_groups=mesh['ba'=2,'row'=4,'col'=4] {'row'}, dimensions={1}, use_global_device_ids=true | all-gather | bytes 983040 | tf_op jit(solution)/shard_map/all_gather | solution.py:204
  211.6 38.8 %all-gather.8.cloned.1.call-done = bf16[1536,768]{1,0:T(8,128)(2,1)} async-done(((bf16[384,768]{1,0:T(8,128)(2,1)}), bf16[1536,768]{1,0:T(8,128)(2,1)}) %all-gather.8.cloned.1.call-update) | async-done | bytes 2359312 | tf_op jit(solution)/shard_map/all_gather | solution.py:51
  257.8 42.7 %all-gather.12.cloned.1.call-done = bf16[1536,768]{1,0:T(8,128)(2,1)} async-done(((bf16[384,768]{1,0:T(8,128)(2,1)}), bf16[1536,768]{1,0:T(8,128)(2,1)}) %all-gather.12.cloned.1.call-update) | async-done | bytes 2359312 | tf_op jit(solution)/shard_map/all_gather | solution.py:59
  313.0 83.8 %reduce-scatter.15.cloned.1.call-done = f32[384,768]{1,0:T(8,128)} async-done(((f32[1536,768]{1,0:T(8,128)}), f32[384,768]{1,0:T(8,128)}) %reduce-scatter.15.cloned.1.call-update) | async-done | bytes 1179664 | tf_op jit(solution)/shard_map/reduce_scatter | solution.py:71
  407.7 43.9 %all-gather.14.cloned.1.call-done = bf16[1536,768]{1,0:T(8,128)(2,1)} async-done(((bf16[384,768]{1,0:T(8,128)(2,1)}), bf16[1536,768]{1,0:T(8,128)(2,1)}) %all-gather.14.cloned.1.call-update) | async-done | bytes 2359312 | tf_op jit(solution)/shard_map/all_gather | solution.py:59
  459.1 161.2 %while.29 = (s32[]{:T(128)}, f32[1536,3,64]{0,2,1:T(8,128)}, f32[1536,3,64]{0,2,1:T(8,128)S(1)}, f32[3,512,3,64]{1,0,3,2:T(4,128)}, bf16[3,512,3,64]{1,3,2,0:T(8...) while((s32[]{:T(128)}, f32[1536,3,64]{0,2,1:T(8,128)}, ...), condition=%wide.region_15.16_spmd.clone, body=%wide.region_13.15_spmd.clone.sunk | while | flops 1546524672 | bytes 133533912 | solution.py:165
  473.3 14.1 %fusion.158 = f32[1,512,3,64]{1,3,2,0:T(8,128)} fusion(bf16[1536,3,64]{0,2,1:T(8,128)(2,1)} %get-tuple-element.572, f32[3,512,1536]{2,1,0:T(8,128)} %copy-done, f32[3,512,1536]{2,1,0:T(8,128)} %fusion.155), kind=kOutput, calls=%fused_computation.36.clone.1 | convolution fusion | flops 313789440 | bytes 19857408 | tf_op jit(solution)/shard_map/while/body/eval_jaxpr/hqk,khd->qhd/dot_general | solution.py:150
  487.3 15.3 %fusion.156 = f32[1536,3,64]{0,2,1:T(8,128)} fusion(f32[3,512,1536]{2,1,0:T(8,128)} %copy-done, f32[3,512,1536]{2,1,0:T(8,128)} %fusion.155, f32[1536,3,64]{0,2,1:T(8,128)} %get-tuple-element.551, pred[]{:T(512)S(6)} %compare.3, bf16[3,512,3,64]{1,3,2,0:T(8,128)(2,1)} %get-tuple-element.568, s32[]{:T(128)S(6)} %copy.72), kind=kOutput, calls=%fused_computation.35.clone.1 | convolution fusion | flops 314379264 | bytes 40304644 | tf_op jit(solution)/shard_map/while/body/eval_jaxpr/hqk,qhd->khd/dot_general | solution.py:153
  504.1 8.6 dynamic_update_slice.21
  526.8 14.1 %fusion.158 = f32[1,512,3,64]{1,3,2,0:T(8,128)} fusion(bf16[1536,3,64]{0,2,1:T(8,128)(2,1)} %get-tuple-element.572, f32[3,512,1536]{2,1,0:T(8,128)} %copy-done, f32[3,512,1536]{2,1,0:T(8,128)} %fusion.155), kind=kOutput, calls=%fused_computation.36.clone.1 | convolution fusion | flops 313789440 | bytes 19857408 | tf_op jit(solution)/shard_map/while/body/eval_jaxpr/hqk,khd->qhd/dot_general | solution.py:150
  540.9 15.6 %fusion.156 = f32[1536,3,64]{0,2,1:T(8,128)} fusion(f32[3,512,1536]{2,1,0:T(8,128)} %copy-done, f32[3,512,1536]{2,1,0:T(8,128)} %fusion.155, f32[1536,3,64]{0,2,1:T(8,128)} %get-tuple-element.551, pred[]{:T(512)S(6)} %compare.3, bf16[3,512,3,64]{1,3,2,0:T(8,128)(2,1)} %get-tuple-element.568, s32[]{:T(128)S(6)} %copy.72), kind=kOutput, calls=%fused_computation.35.clone.1 | convolution fusion | flops 314379264 | bytes 40304644 | tf_op jit(solution)/shard_map/while/body/eval_jaxpr/hqk,qhd->khd/dot_general | solution.py:153
  557.9 8.6 dynamic_update_slice.21
  580.6 14.1 %fusion.158 = f32[1,512,3,64]{1,3,2,0:T(8,128)} fusion(bf16[1536,3,64]{0,2,1:T(8,128)(2,1)} %get-tuple-element.572, f32[3,512,1536]{2,1,0:T(8,128)} %copy-done, f32[3,512,1536]{2,1,0:T(8,128)} %fusion.155), kind=kOutput, calls=%fused_computation.36.clone.1 | convolution fusion | flops 313789440 | bytes 19857408 | tf_op jit(solution)/shard_map/while/body/eval_jaxpr/hqk,khd->qhd/dot_general | solution.py:150
  594.7 15.7 %fusion.156 = f32[1536,3,64]{0,2,1:T(8,128)} fusion(f32[3,512,1536]{2,1,0:T(8,128)} %copy-done, f32[3,512,1536]{2,1,0:T(8,128)} %fusion.155, f32[1536,3,64]{0,2,1:T(8,128)} %get-tuple-element.551, pred[]{:T(512)S(6)} %compare.3, bf16[3,512,3,64]{1,3,2,0:T(8,128)(2,1)} %get-tuple-element.568, s32[]{:T(128)S(6)} %copy.72), kind=kOutput, calls=%fused_computation.35.clone.1 | convolution fusion | flops 314379264 | bytes 40304644 | tf_op jit(solution)/shard_map/while/body/eval_jaxpr/hqk,qhd->khd/dot_general | solution.py:153
  654.6 35.2 %reduce-scatter.19.cloned.1.call-done = f32[192,576]{1,0:T(8,128)} async-done(((f32[768,576]{1,0:T(8,128)}), f32[192,576]{1,0:T(8,128)}) %reduce-scatter.19.cloned.1.call-update) | async-done | bytes 442384 | tf_op jit(solution)/shard_map/reduce_scatter | solution.py:63
  691.8 31.8 %reduce-scatter.23.cloned.1.call-done = f32[512,192]{0,1:T(8,128)} async-done(((f32[512,768]{0,1:T(8,128)}), f32[512,192]{0,1:T(8,128)}) %reduce-scatter.23.cloned.1.call-update) | async-done | bytes 393232 | tf_op jit(solution)/shard_map/reduce_scatter | solution.py:67
  723.6 87.3 %reduce-scatter.17.cloned.1.call-done = f32[384,768]{1,0:T(8,128)} async-done(((f32[1536,768]{1,0:T(8,128)}), f32[384,768]{1,0:T(8,128)}) %reduce-scatter.17.cloned.1.call-update) | async-done | bytes 1179664 | tf_op jit(solution)/shard_map/reduce_scatter | solution.py:71
  813.2 44.3 %all-reduce = (f32[768]{0:T(1024)}, f32[768]{0:T(1024)}) all-reduce(f32[768]{0:T(1024)} %get-tuple-element.276, f32[768]{0:T(1024)} %get-tuple-element.274), channel_id=1, replica_groups=mesh['ba'=2,'row'=4,'col'=4] {'ba','row','col'}, use_global_device_ids=true, to_apply=%region_30.31 | all-reduce | flops 1536 | bytes 12288 | tf_op jit(solution)/shard_map/psum | solution.py:275
  858.8 41.2 %reduce-scatter.13.cloned.1.call-done = f32[384,768]{1,0:T(8,128)} async-done(((f32[1536,768]{1,0:T(8,128)}), f32[384,768]{1,0:T(8,128)}) %reduce-scatter.13.cloned.1.call-update) | async-done | bytes 1179664 | tf_op jit(solution)/shard_map/reduce_scatter | solution.py:71
  (241 shorter events, 204.8 us)
Async XLA Ops:
  8.1 56.9 %all-gather.6.cloned.1.call-start = ((), (), s32[]{:S(2)}) async-start(), calls=%async_computation.8 | async-start | bytes 2949120 | tf_op jit(solution)/shard_map/all_gather | solution.py:51
  11.6 185.6 %reduce-scatter.11.cloned.1.call-start = ((), (), s32[]{:S(2)}) async-start(), calls=%async_computation.9 | async-start | bytes 5898240 | tf_op jit(solution)/shard_map/reduce_scatter | solution.py:71
  113.0 84.3 %copy-start.1 = (bf16[384,768]{1,0:T(8,128)(2,1)S(1)}, bf16[384,768]{1,0:T(8,128)(2,1)}, u32[]{:S(2)}) copy-start(bf16[384,768]{1,0:T(8,128)(2,1)} %param.16) | copy-start | bytes 1769476
  113.0 85.7 %copy-start.34 = (f32[768]{0:T(1024)S(1)}, f32[768]{0:T(1024)}, u32[]{:S(2)}) copy-start(f32[768]{0:T(1024)} %param.26) | copy-start | bytes 9220
  113.0 98.6 %all-gather.10.cloned.1.call-start = ((), (), s32[]{:S(2)}) async-start(), calls=%async_computation.11 | async-start | bytes 1966080 | tf_op jit(solution)/shard_map/all_gather | solution.py:200
  114.8 85.6 %copy-start.27 = (bf16[512,192]{0,1:T(8,128)(2,1)S(1)}, bf16[512,192]{0,1:T(8,128)(2,1)}, u32[]{:S(2)}) copy-start(bf16[512,192]{0,1:T(8,128)(2,1)} %param.24) | copy-start | bytes 589828
  114.8 135.6 %all-gather.8.cloned.1.call-start = ((), (), s32[]{:S(2)}) async-start(), calls=%async_computation.10 | async-start | bytes 2949120 | tf_op jit(solution)/shard_map/all_gather | solution.py:51
  199.8 100.8 %all-gather.12.cloned.1.call-start = ((), (), s32[]{:S(2)}) async-start(), calls=%async_computation.13 | async-start | bytes 2949120 | tf_op jit(solution)/shard_map/all_gather | solution.py:59
  200.3 196.5 %reduce-scatter.15.cloned.1.call-start = ((), (), s32[]{:S(2)}) async-start(), calls=%async_computation.14 | async-start | bytes 5898240 | tf_op jit(solution)/shard_map/reduce_scatter | solution.py:71
  211.6 88.9 %copy-start.8 = (bf16[512,768]{0,1:T(8,128)(2,1)}, bf16[512,768]{0,1:T(8,128)(2,1)S(1)}, u32[]{:S(2)}) copy-start(bf16[512,768]{0,1:T(8,128)(2,1)S(1)} %all_gather.31) | copy-start | bytes 2359300
  313.0 86.2 %copy-start.5 = (bf16[384,768]{1,0:T(8,128)(2,1)S(1)}, bf16[384,768]{1,0:T(8,128)(2,1)}, u32[]{:S(2)}) copy-start(bf16[384,768]{1,0:T(8,128)(2,1)} %param.27) | copy-start | bytes 1769476
  313.0 138.5 %all-gather.14.cloned.1.call-start = ((), (), s32[]{:S(2)}) async-start(), calls=%async_computation.15 | async-start | bytes 2949120 | tf_op jit(solution)/shard_map/all_gather | solution.py:59
  400.3 249.3 %reduce-scatter.21.cloned.1.call-start = ((), (), s32[]{:S(2)}) async-start(), calls=%async_computation.18 | async-start | bytes 3932160 | tf_op jit(solution)/shard_map/reduce_scatter | solution.py:63
  407.4 245.5 %reduce-scatter.25.cloned.1.call-start = ((), (), s32[]{:S(2)}) async-start(), calls=%async_computation.20 | async-start | bytes 983040
  628.0 61.8 %reduce-scatter.19.cloned.1.call-start = ((), (), s32[]{:S(2)}) async-start(), calls=%async_computation.17 | async-start | bytes 2457600 | tf_op jit(solution)/shard_map/reduce_scatter | solution.py:63
  634.5 89.0 %reduce-scatter.23.cloned.1.call-start = ((), (), s32[]{:S(2)}) async-start(), calls=%async_computation.19 | async-start | bytes 1966080 | tf_op jit(solution)/shard_map/reduce_scatter | solution.py:67
  638.9 172.0 %reduce-scatter.17.cloned.1.call-start = ((), (), s32[]{:S(2)}) async-start(), calls=%async_computation.16 | async-start | bytes 5898240 | tf_op jit(solution)/shard_map/reduce_scatter | solution.py:71
  644.8 255.2 %reduce-scatter.13.cloned.1.call-start = ((), (), s32[]{:S(2)}) async-start(), calls=%async_computation.12 | async-start | bytes 5898240 | tf_op jit(solution)/shard_map/reduce_scatter | solution.py:71
  649.5 161.4 %copy-start.2 = (bf16[384,768]{1,0:T(8,128)(2,1)S(1)}, bf16[384,768]{1,0:T(8,128)(2,1)}, u32[]{:S(2)}) copy-start(bf16[384,768]{1,0:T(8,128)(2,1)} %param.16) | copy-start | bytes 1769476
  649.5 161.4 %copy-start.35 = (f32[768]{0:T(1024)S(1)}, f32[768]{0:T(1024)}, u32[]{:S(2)}) copy-start(f32[768]{0:T(1024)} %param.25) | copy-start | bytes 9220
  649.5 161.4 %copy-start.37 = (f32[384]{0:T(512)S(1)}, f32[384]{0:T(512)}, u32[]{:S(2)}) copy-start(f32[384]{0:T(512)} %copy-done.36) | copy-start | bytes 4612
  649.6 253.6 %all-reduce.4.cloned.1.call-start = ((), (), s32[]{:S(2)}) async-start(), calls=%async_computation.21 | async-start | bytes 3932160 | tf_op jit(solution)/shard_map/psum | solution.py:272
  654.6 245.4 %copy-start.4 = (f32[384,768]{1,0:T(8,128)S(1)}, f32[384,768]{1,0:T(8,128)}, u32[]{:S(2)}) copy-start(f32[384,768]{1,0:T(8,128)} %reduce-scatter.15.cloned.1.call-done) | copy-start | bytes 3538948
  654.6 245.4 %copy-start.6 = (bf16[384,768]{1,0:T(8,128)(2,1)S(1)}, bf16[384,768]{1,0:T(8,128)(2,1)}, u32[]{:S(2)}) copy-start(bf16[384,768]{1,0:T(8,128)(2,1)} %param.27) | copy-start | bytes 1769476
  (41 other events, 226.2 us)
Sparse Core Ops, SparseCore 0:
  11.7 53.1 all-gather.5
  113.1 84.0 reduce-scatter.10
  400.5 50.9 all-gather.13
  723.7 21.5 all-reduce.3
Sparse Core Ops, SparseCore 1:
  115.9 29.6 all-gather.9
  199.9 50.5 all-gather.7
  251.8 48.6 all-gather.11
  313.0 83.8 reduce-scatter.14
  407.5 44.3 reduce-scatter.20
  628.0 24.8 reduce-scatter.24
  655.8 33.9 reduce-scatter.18
  692.7 30.8 reduce-scatter.22
  725.7 85.1 reduce-scatter.16
  813.2 86.7 reduce-scatter.12
where the time goes:
time: 931 us; the launch traced here: 921 us
  waiting for transfers between devices  515 us (55%)
  matrix products  200 us (21%)
  blocking collectives  79.7 us (9%)
  local copies, waits for them, and re-layouts  69.4 us (7%)
  other arithmetic  38.2 us (4%)
  between operations  16.3 us (2%)
    reduce_scatter x4, waiting for transfers between devices, reduce_cols(): lax.psum_scatter(contract(block_rows, weight_local, 1, 1 if flipped else...  295 us
    all_gather x2, waiting for transfers between devices, spread_grads(): return lax.all_gather(values, 'col', axis=0, tiled=True)  86.6 us
    all_gather x2, waiting for transfers between devices, spread_normed(): return lax.all_gather(values, 'col', axis=0, tiled=True)  65.1 us
    dot_general x11, matrix products, contract(): lax.dot_general(left, right, (((first,), (second,)), ((), ())), preferred...  51.7 us
    dot_general x3, matrix products, one_block(): jnp.einsum('hqk,qhd->khd', grad_raw, query_block, preferred_element_type=...  46.6 us
    psum x1, blocking collectives, shards(): lax.psum((gain_attn_part, gain_mlp_part), ('ba', 'row', 'col'))  44.3 us
    dot_general x3, matrix products, one_block(): jnp.einsum('hqk,khd->qhd', grad_raw, key_rot, preferred_element_type=jnp....  42.2 us
    reduce_scatter x2, waiting for transfers between devices, rows_in(): return lax.psum_scatter(values, 'row', scatter_dimension=0, tiled=True)  35.2 us
  transfers between devices with their start and end apart: 14, of which 11 were waited for; matrix products, arithmetic and copies ran while one was open for 24% of the time, Pallas kernels for 0%

commit v1 on v0

v1 whole, which is shorter than its diff:
```python
import functools
import jax
import jax.numpy as jnp
from jax import lax
from jax.experimental import pallas as pl
from jax.experimental.pallas import tpu as pltpu
from jax.sharding import PartitionSpec as P

HEAD_DIM = 64
PAIR = 2 * HEAD_DIM
LONGEST = 768
EPSILON = 1e-06
ROPE_BASE = 10000.0
Q_ROWS = 128
NEG = -1e30


def contract(left, right, first, second):
    return lax.dot_general(
        left, right, (((first,), (second,)), ((), ())), preferred_element_type=jnp.float32
    )


def seq_starts(lengths, places):
    starts = jnp.zeros_like(places)
    end = jnp.int32(0)
    for j in range(len(lengths)):
        end = end + lengths[j]
        starts = jnp.where(places >= end, end, starts)
    return starts


def split_heads(pair):
    lane = lax.broadcasted_iota(jnp.int32, pair.shape, 1)
    zero = jnp.zeros_like(pair)
    return jnp.concatenate(
        [jnp.where(lane < HEAD_DIM, pair, zero), jnp.where(lane >= HEAD_DIM, pair, zero)], axis=0
    )


def join_heads(stacked):
    rows = stacked.shape[0] // 2
    lane = lax.broadcasted_iota(jnp.int32, (rows, PAIR), 1)
    return jnp.where(lane < HEAD_DIM, stacked[:rows], stacked[rows:])


def attend_forward_kernel(seqs, len_ref, q_ref, k_ref, v_ref, o_ref):
    step = pl.program_id(0)
    halo = k_ref.shape[0] - pl.num_programs(0) * Q_ROWS
    window = halo + Q_ROWS
    first_query = len_ref[seqs] + step * Q_ROWS
    lengths = [len_ref[j] for j in range(seqs)]
    query_place = first_query + lax.broadcasted_iota(jnp.int32, (Q_ROWS, 1), 0)
    start = seq_starts(lengths, query_place)
    key_place = first_query - halo + lax.broadcasted_iota(jnp.int32, (Q_ROWS, window), 1)
    bias = jnp.where((key_place >= start) & (key_place <= query_place), 0.0, NEG)
    bias = jnp.concatenate([bias, bias], axis=0)
    first = pl.multiple_of(step * Q_ROWS, Q_ROWS)
    for pair in range(q_ref.shape[1] // PAIR):
        lanes = slice(pair * PAIR, (pair + 1) * PAIR)
        query = split_heads(q_ref[:, lanes] * HEAD_DIM ** (-0.5))
        keys = k_ref[pl.ds(first, window), lanes]
        scores = contract(query, keys, 1, 1) + bias
        peak = jnp.max(scores, axis=1, keepdims=True)
        weights = jnp.exp(scores - peak)
        total = jnp.sum(weights, axis=1, keepdims=True)
        out = contract(weights.astype(jnp.bfloat16), v_ref[pl.ds(first, window), lanes], 1, 0)
        o_ref[:, lanes] = join_heads(out / total).astype(o_ref.dtype)


def attend_backward_kernel(seqs, len_ref, q_ref, k_ref, v_ref, g_ref, dq_ref, dk_ref, dv_ref):
    step = pl.program_id(0)
    halo = k_ref.shape[0] - pl.num_programs(0) * Q_ROWS
    window = halo + Q_ROWS
    first_query = len_ref[seqs] + step * Q_ROWS
    lengths = [len_ref[j] for j in range(seqs)]
    query_place = first_query + lax.broadcasted_iota(jnp.int32, (1, Q_ROWS), 1)
    start = seq_starts(lengths, query_place)
    key_place = first_query - halo + lax.broadcasted_iota(jnp.int32, (window, Q_ROWS), 0)
    bias = jnp.where((key_place >= start) & (key_place <= query_place), 0.0, NEG)
    bias = jnp.concatenate([bias, bias], axis=1)
    first = pl.multiple_of(step * Q_ROWS, Q_ROWS)

    @pl.when(step == 0)
    def _():
        dk_ref[...] = jnp.zeros_like(dk_ref)
        dv_ref[...] = jnp.zeros_like(dv_ref)

    for pair in range(q_ref.shape[1] // PAIR):
        lanes = slice(pair * PAIR, (pair + 1) * PAIR)
        query = split_heads(q_ref[:, lanes] * HEAD_DIM ** (-0.5))
        grad = split_heads(g_ref[:, lanes])
        keys = k_ref[pl.ds(first, window), lanes]
        scores = contract(keys, query, 1, 1) + bias
        weights = jnp.exp(scores - jnp.max(scores, axis=0, keepdims=True))
        probs = weights * (1.0 / jnp.sum(weights, axis=0, keepdims=True))
        grad_probs = contract(v_ref[pl.ds(first, window), lanes], grad, 1, 1)
        inner = jnp.sum(probs * grad_probs, axis=0, keepdims=True)
        grad_raw = (probs * (grad_probs - inner)).astype(jnp.bfloat16)
        dv_ref[pl.ds(first, window), lanes] += contract(probs.astype(jnp.bfloat16), grad, 1, 0)
        dk_ref[pl.ds(first, window), lanes] += contract(grad_raw, query, 1, 0)
        dq_ref[:, lanes] = join_heads(contract(grad_raw, keys, 0, 0)) * HEAD_DIM ** (-0.5)


VMEM_LIMIT = 48 * 1024 * 1024


def attend_forward(info, query, keys, values):
    rows, width = query.shape
    whole = pl.BlockSpec(keys.shape, lambda i: (0, 0))
    part = pl.BlockSpec((Q_ROWS, width), lambda i: (i, 0))
    return pl.pallas_call(
        functools.partial(attend_forward_kernel, info.shape[0] - 1),
        out_shape=jax.ShapeDtypeStruct(query.shape, jnp.bfloat16),
        grid=(rows // Q_ROWS,),
        in_specs=[pl.BlockSpec(memory_space=pltpu.SMEM), part, whole, whole],
        out_specs=part,
        compiler_params=pltpu.CompilerParams(vmem_limit_bytes=VMEM_LIMIT),
        name="attend_forward",
    )(info, query, keys, values)


def attend_backward(info, query, keys, values, grads):
    rows, width = query.shape
    whole = pl.BlockSpec(keys.shape, lambda i: (0, 0))
    part = pl.BlockSpec((Q_ROWS, width), lambda i: (i, 0))
    return pl.pallas_call(
        functools.partial(attend_backward_kernel, info.shape[0] - 1),
        out_shape=(
            jax.ShapeDtypeStruct(query.shape, jnp.float32),
            jax.ShapeDtypeStruct(keys.shape, jnp.float32),
            jax.ShapeDtypeStruct(keys.shape, jnp.float32),
        ),
        grid=(rows // Q_ROWS,),
        in_specs=[pl.BlockSpec(memory_space=pltpu.SMEM), part, whole, whole, part],
        out_specs=(part, whole, whole),
        compiler_params=pltpu.CompilerParams(vmem_limit_bytes=VMEM_LIMIT),
        name="attend_backward",
    )(info, query, keys, values, grads)


def rotate(values, angles, direction):
    half = HEAD_DIM // 2
    rows = values.shape[0]
    cosine = jnp.cos(angles)[:, None, :]
    sine = jnp.sin(angles)[:, None, :]
    heads = values.reshape(rows, -1, HEAD_DIM)
    front, back = heads[..., :half], heads[..., half:]
    return jnp.concatenate(
        [
            front * cosine - direction * back * sine,
            back * cosine + direction * front * sine,
        ],
        axis=-1,
    ).reshape(values.shape)


def norm_forward(values, gain):
    scale = lax.rsqrt(jnp.mean(values * values, axis=1, keepdims=True) + EPSILON)
    return scale, values * scale * gain[None, :]


def norm_backward(values, scale, gain, grad_normed):
    weighted = grad_normed * gain[None, :]
    inner = jnp.mean(weighted * values, axis=1, keepdims=True)
    grad_values = scale * weighted - values * (scale**3 * inner)
    return grad_values, jnp.sum(grad_normed * values * scale, axis=0)


def gather_in(weight):
    return lax.all_gather(
        lax.all_gather(weight, "col", axis=1, tiled=True), "row", axis=0, tiled=True
    )


def gather_out(weight):
    return lax.all_gather(
        lax.all_gather(weight, "col", axis=0, tiled=True), "row", axis=1, tiled=True
    )


def scatter_in(grad):
    part = lax.psum_scatter(grad, "ba", scatter_dimension=0, tiled=True)
    return part


def shards(
    n_row, n_col, tokens, lengths, w_query, w_key, w_value, w_out, w_gate, w_up, w_down,
    gain_attn, gain_mlp, cotangent,
):
    low = jnp.bfloat16
    rows, width = tokens.shape
    col = lax.axis_index("col")
    hops = -(-(LONGEST - 1) // rows)
    step_right = [(i, i + 1) for i in range(n_col - 1)]
    step_left = [(i + 1, i) for i in range(n_col - 1)]

    blocks = [tokens]
    for _ in range(hops):
        blocks.insert(0, lax.ppermute(blocks[0], "col", step_right))
    halo = hops * rows
    seen = jnp.concatenate(blocks, axis=0).astype(jnp.float32)

    w_qkv = jnp.stack([w_query, w_key, w_value])
    qkv = lax.all_gather(lax.all_gather(w_qkv, "col", axis=2, tiled=True), "row", axis=1, tiled=True)
    wq, wk, wv = qkv[0], qkv[1], qkv[2]
    wo = gather_out(w_out)
    wgu = lax.all_gather(
        lax.all_gather(jnp.stack([w_gate, w_up]), "col", axis=2, tiled=True), "row", axis=1, tiled=True
    )
    wg, wu = wgu[0], wgu[1]
    wd = gather_out(w_down)

    first = col * rows
    info = jnp.concatenate([lengths[0], first[None]]).astype(jnp.int32)
    place = first - halo + jnp.arange(halo + rows, dtype=jnp.int32)
    seq_list = [lengths[0, j] for j in range(lengths.shape[1])]
    position = (place - seq_starts(seq_list, place)).astype(jnp.float32)
    half = HEAD_DIM // 2
    frequency = ROPE_BASE ** (-jnp.arange(half, dtype=jnp.float32) / half)
    angles = position[:, None] * frequency[None, :]

    scale_seen, normed_seen = norm_forward(seen, gain_attn)
    h1 = normed_seen.astype(low)
    q = rotate(contract(h1[halo:], wq, 1, 0), angles[halo:], 1.0).astype(low)
    k = rotate(contract(h1, wk, 1, 0), angles, 1.0).astype(low)
    v = contract(h1, wv, 1, 0).astype(low)
    heads = attend_forward(info, q, k, v)
    x = tokens.astype(jnp.float32)
    scale_attn = scale_seen[halo:]
    middle = x + contract(heads, wo, 1, 0)
    scale_mlp, normed_mlp = norm_forward(middle, gain_mlp)
    h2 = normed_mlp.astype(low)
    gate = contract(h2, wg, 1, 0)
    up = contract(h2, wu, 1, 0)
    sig = jax.nn.sigmoid(gate)
    silu = gate * sig
    hidden = (silu * up).astype(low)
    layer_out = (middle + contract(hidden, wd, 1, 0)).astype(low)

    grad_hidden = contract(cotangent, wd, 1, 1)
    d_gate = (grad_hidden * up * (sig + silu * (1.0 - sig))).astype(low)
    d_up = (grad_hidden * silu).astype(low)
    d_h2 = contract(d_gate, wg, 1, 1) + contract(d_up, wu, 1, 1)
    d_norm, gain_mlp_part = norm_backward(middle, scale_mlp, gain_mlp, d_h2)
    d_middle = cotangent.astype(jnp.float32) + d_norm
    dm = d_middle.astype(low)

    def reduce_grad(parts, in_side):
        part = lax.psum_scatter(parts, "row", scatter_dimension=1 if in_side else 2, tiled=True)
        part = lax.psum_scatter(part, "col", scatter_dimension=2 if in_side else 1, tiled=True)
        return lax.psum(part.astype(jnp.float32), "ba")

    grad_down = reduce_grad(contract(hidden, cotangent, 0, 0).astype(low)[None], False)[0]
    grad_gu = reduce_grad(
        jnp.stack([contract(h2, d_gate, 0, 0), contract(h2, d_up, 0, 0)]).astype(low), True
    )
    grad_out = reduce_grad(contract(heads, dm, 0, 0).astype(low)[None], False)[0]

    d_heads = contract(dm, wo, 1, 1).astype(low)
    dqr, dkr, dvr = attend_backward(info, q, k, v, d_heads)
    dq = rotate(dqr, angles[halo:], -1.0).astype(low)
    dk = rotate(dkr, angles, -1.0).astype(low)
    dv = dvr.astype(low)
    d_seen = contract(dk, wk, 1, 1) + contract(dv, wv, 1, 1)
    d_h1 = contract(dq, wq, 1, 1) + d_seen[halo:]
    travelling = d_seen[:rows].astype(low)
    for hop in range(hops):
        arrived = lax.ppermute(travelling, "col", step_left).astype(jnp.float32)
        if hop + 1 < hops:
            travelling = (d_seen[(hop + 1) * rows : (hop + 2) * rows] + arrived).astype(low)
        else:
            d_h1 = d_h1 + arrived
    grad_qkv = reduce_grad(
        jnp.stack(
            [contract(h1[halo:], dq, 0, 0), contract(h1, dk, 0, 0), contract(h1, dv, 0, 0)]
        ).astype(low),
        True,
    )
    d_norm, gain_attn_part = norm_backward(x, scale_attn, gain_attn, d_h1)
    input_grad = (d_middle + d_norm).astype(low)
    grad_gain_attn, grad_gain_mlp = lax.psum((gain_attn_part, gain_mlp_part), ("ba", "row", "col"))
    return (
        layer_out, input_grad, grad_qkv[0], grad_qkv[1], grad_qkv[2], grad_out, grad_gu[0],
        grad_gu[1], grad_down, grad_gain_attn, grad_gain_mlp,
    )


def solution(mesh):
    tokens = P(("ba", "row", "col"), None)
    in_side, out_side = P("row", "col"), P("col", "row")
    in_specs = (
        tokens, P(("ba", "row"), None), in_side, in_side, in_side, out_side, in_side, in_side,
        out_side, P(), P(), tokens,
    )
    out_specs = (
        tokens, tokens, in_side, in_side, in_side, out_side, in_side, in_side, out_side, P(), P(),
    )
    body = functools.partial(shards, mesh.shape["row"], mesh.shape["col"])
    return jax.shard_map(
        body, mesh=mesh, in_specs=in_specs, out_specs=out_specs, check_vma=False
    )
```

time: 931 us -> 667 us (0.72)
  waiting for transfers between devices: 515 us -> 288 us
  matrix products: 200 us -> 62.6 us
  blocking collectives: 79.7 us -> 143 us
  Pallas kernels: 0 us -> 35.6 us
  other arithmetic: 38.2 us -> 22.9 us
  starting transfers between devices: 1.24 us -> 10.8 us
    reduce_scatter x7 -> x5, waiting for transfers between devices: 362 us -> 141 us  [the longest x2 115 us: reduce_grad(): lax.psum_scatter(parts, 'row', scatter_dimension=1 if in_side else 2, til...]
    dot_general x21 -> x0, matrix products: 145 us -> none  [the longest x3 46.6 us: one_block(): jnp.einsum('hqk,qhd->khd', grad_raw, query_block, preferred_element_type=...]
    all_gather x3, blocking collectives: 35.4 us -> 95.2 us  [the longest x1 52.3 us: shards(): lax.all_gather(w_qkv, 'col', axis=2, tiled=True)]
    all_gather x5, waiting for transfers between devices: 152 us -> 94.1 us  [the longest x1 56.8 us: shards(): lax.all_gather(lax.all_gather(jnp.stack([w_gate, w_up]), 'col', axis=2, t...]
    ppermute x0 -> x4, waiting for transfers between devices: none -> 45.4 us  [the longest x2 40.2 us: shards(): arrived = lax.ppermute(travelling, 'col', step_left).astype(jnp.float32)]
    pallas_call x0 -> x2, Pallas kernels: none -> 35.6 us  [the longest x1 25 us: attend_backward(): pl.pallas_call(functools.partial(attend_backward_kernel, info.shape[0] -...]
    unnamed x96 -> x108, local copies, waits for them, and re-layouts: 19.5 us -> 54.9 us
    dynamic_update_slice x6 -> x0, local copies, waits for them, and re-layouts: 30 us -> none  [attention_forward(): lax.map(one_block, (query_rot.reshape(blocks, block_rows, query_rot.shape...]
  transfers between devices with their start and end apart: 14 -> 18, of which waited for: 11 -> 9; matrix products, arithmetic and copies ran while one was open for 24% -> 19% of each run, Pallas kernels for 0% -> 5%
where the time goes in v1:
time: 667 us; the launch traced here: 656 us
  waiting for transfers between devices  288 us (43%)
  blocking collectives  143 us (21%)
  local copies, waits for them, and re-layouts  75.1 us (11%)
  matrix products  62.6 us (9%)
  Pallas kernels  35.6 us (5%)
  other arithmetic  22.9 us (3%)
  between operations  17.7 us (3%)
  starting transfers between devices  10.8 us (2%)
    reduce_scatter x2, waiting for transfers between devices, reduce_grad(): lax.psum_scatter(parts, 'row', scatter_dimension=1 if in_side else 2, til...  115 us
    dot_general x21, matrix products, contract(): lax.dot_general(left, right, (((first,), (second,)), ((), ())), preferred...  62.6 us
    all_gather x1, waiting for transfers between devices, shards(): lax.all_gather(lax.all_gather(jnp.stack([w_gate, w_up]), 'col', axis=2, t...  56.8 us
    unnamed x108, local copies, waits for them, and re-layouts  54.9 us
    all_gather x1, blocking collectives, shards(): lax.all_gather(w_qkv, 'col', axis=2, tiled=True)  52.3 us
    all_gather x2, blocking collectives, gather_out(): lax.all_gather(weight, 'col', axis=0, tiled=True)  42.8 us
    psum x1, blocking collectives, shards(): lax.psum((gain_attn_part, gain_mlp_part), ('ba', 'row', 'col'))  40.5 us
    ppermute x2, waiting for transfers between devices, shards(): arrived = lax.ppermute(travelling, 'col', step_left).astype(jnp.float32)  40.2 us
  transfers between devices with their start and end apart: 18, of which 9 were waited for; matrix products, arithmetic and copies ran while one was open for 19% of the time, Pallas kernels for 5%

profile of v1, /device:TPU:0, one launch (start us, length us, event | category | flops | bytes accessed | tf_op | source)
XLA Modules:
  0.0 656.2 jit_solution(16165507096136076924)
XLA Ops:
  10.4 52.3 %all_gather.24 = bf16[3,192,768]{1,0,2:T(4,128)(2,1)S(1)} all-gather(bf16[3,192,192]{1,0,2:T(4,128)(2,1)S(1)} %copy.64), channel_id=1, replica_groups=mesh['ba'=2,'row'=4,'col'=4] {'col'}, dimensions={2}, use_global_device_ids=true | all-gather | bytes 1105920 | tf_op jit(solution)/shard_map/all_gather | solution.py:205
  64.9 15.9 %all_gather.26 = bf16[768,192]{1,0:T(8,128)(2,1)S(1)} all-gather(bf16[192,192]{1,0:T(8,128)(2,1)S(1)} %copy-done.32), channel_id=1, replica_groups=mesh['ba'=2,'row'=4,'col'=4] {'col'}, dimensions={0}, use_global_device_ids=true | all-gather | bytes 368640 | tf_op jit(solution)/shard_map/all_gather | solution.py:178
  85.3 27.0 %all_gather.30 = bf16[2048,192]{0,1:T(8,128)(2,1)} all-gather(bf16[512,192]{0,1:T(8,128)(2,1)S(1)} %copy-done.30), channel_id=1, replica_groups=mesh['ba'=2,'row'=4,'col'=4] {'col'}, dimensions={0}, use_global_device_ids=true | all-gather | bytes 983040 | tf_op jit(solution)/shard_map/all_gather | solution.py:178
  122.4 5.3 collective-permute-done.1
  145.6 10.6 %attend_forward.1 = bf16[384,768]{1,0:T(8,128)(2,1)S(1)} custom-call(s32[5]{0:T(128)S(1)} %pad_add_fusion.len_ref, bf16[384,768]{1,0:T(8,128)(2,1)S(1)} %copy-done, bf16[1152,768]{1,0:T(8,128)(2,1)S(1)} %copy.69.k_ref, bf16[1152,768]{1,0:T(8,128)(2,1)S(1)} %convolution_convert_fusion.3.v_ref), custom_call_target="tpu_custom_call" | custom-call | tf_op jit(solution)/shard_map/attend_forward/pallas_call | solution.py:112
  161.7 56.8 %all-gather.12.cloned.1.call-done = bf16[2,768,2048]{2,1,0:T(8,128)(2,1)} async-done(((bf16[2,192,2048]{2,1,0:T(8,128)(2,1)}), bf16[2,768,2048]{2,1,0:T(8,128)(2,1)}) %all-gather.12.cloned.1.call-update) | async-done | bytes 6291472 | tf_op jit(solution)/shard_map/all_gather | solution.py:208
  218.5 5.2 fusion.9
  226.9 37.3 %all-gather.14.cloned.1.call-done = bf16[2048,768]{0,1:T(8,128)(2,1)} async-done(((bf16[2048,192]{0,1:T(8,128)(2,1)}), bf16[2048,768]{0,1:T(8,128)(2,1)}) %all-gather.14.cloned.1.call-update) | async-done | bytes 3145744 | tf_op jit(solution)/shard_map/all_gather | solution.py:177
  264.2 7.2 %multiply_convert_fusion = (bf16[384,2048]{1,0:T(8,128)(2,1)S(1)}, bf16[384,2048]{1,0:T(8,128)(2,1)S(1)}, bf16[384,2048]{1,0:T(8,128)(2,1)}) fusion(f32[384,2048]{1,0:T(8,128)} %fusion.7, f32[384,2048]{1,0:T(8,128)} %fusion.9, bf16[384,768]{1,0:T(8,128)(2,1)} %param.23, bf16[2048,768]{0,1:T(8,128)(2,1)} %all-gather.14.cloned.1.call-done), kind=kOutput, calls=%fused_computation.16 | convolution fusion | flops 1218969600 | bytes 14745600 | tf_op jit(solution)/shard_map/dot_general | solution.py:19
  271.4 4.5 fusion.6
  276.0 4.2 multiply_reduce_fusion
  283.5 6.7 %copy.78 = bf16[1,768,768]{1,0,2:T(2,128)(2,1)} copy(bf16[1,768,768]{2,1,0:T(8,128)(2,1)} %fusion.14) | data formatting | bytes 2359296
  293.1 5.2 fusion.5
  298.2 15.9 %copy.80 = bf16[1,2048,768]{1,0,2:T(2,128)(2,1)} copy(bf16[1,2048,768]{2,1,0:T(8,128)(2,1)} %fusion.5) | data formatting | bytes 6291456
  314.1 6.6 %copy.86 = bf16[768,1,2048]{2,0,1:T(8,128)(2,1)} copy(bf16[768,1,2048]{2,1,0:T(2,128)(2,1)} %bitcast.126) | data formatting | bytes 6291456
  323.1 25.0 %attend_backward.1 = (f32[384,768]{1,0:T(8,128)S(1)}, f32[1152,768]{1,0:T(8,128)}, f32[1152,768]{1,0:T(8,128)}) custom-call(s32[5]{0:T(128)S(1)} %pad_add_fusion.len_ref, bf16[384,768]{1,0:T(8,128)(2,1)S(1)} %copy-done.1, bf16[1152,768]{1,0:T(8,128)(2,1)S(1)} %copy.69.k_ref, bf16[1152,768]{1,0:T(8,128)(2,1)S(1)} %convolution_convert_fusion.3.v_ref, ...), custom_call_target="tpu_custom_call" | custom-call | tf_op jit(solution)/shard_map/attend_backward/pallas_call | solution.py:127
  361.9 6.8 %reduce-scatter.29.cloned.1.call-done = bf16[192,2048]{1,0:T(8,128)(2,1)} async-done(((bf16[768,2048]{1,0:T(8,128)(2,1)}), bf16[192,2048]{1,0:T(8,128)(2,1)}) %reduce-scatter.29.cloned.1.call-update) | async-done | bytes 786448
  393.9 26.2 %reduce-scatter.23.cloned.1.call-done = bf16[1,512,192]{2,1,0:T(8,128)(2,1)} async-done(((bf16[1,2048,192]{2,1,0:T(8,128)(2,1)}), bf16[1,512,192]{2,1,0:T(8,128)(2,1)}) %reduce-scatter.23.cloned.1.call-update) | async-done | bytes 196624 | tf_op jit(solution)/shard_map/reduce_scatter | solution.py:251
  421.9 47.0 %reduce-scatter.15.cloned.1.call-done = bf16[3,192,768]{2,1,0:T(8,128)(2,1)} async-done(((bf16[3,768,768]{2,1,0:T(8,128)(2,1)}), bf16[3,192,768]{2,1,0:T(8,128)(2,1)}) %reduce-scatter.15.cloned.1.call-update) | async-done | bytes 884752 | tf_op jit(solution)/shard_map/reduce_scatter | solution.py:250
  474.0 68.0 %reduce-scatter.19.cloned.1.call-done = bf16[2,192,2048]{2,1,0:T(8,128)(2,1)} async-done(((bf16[2,768,2048]{2,1,0:T(8,128)(2,1)}), bf16[2,192,2048]{2,1,0:T(8,128)(2,1)}) %reduce-scatter.19.cloned.1.call-update) | async-done | bytes 1572880 | tf_op jit(solution)/shard_map/reduce_scatter | solution.py:250
  548.7 15.7 %collective-permute-done.2 = bf16[384,768]{1,0:T(8,128)(2,1)S(1)} collective-permute-done((bf16[384,768]{1,0:T(8,128)(2,1)S(1)}, bf16[384,768]{1,0:T(8,128)(2,1)S(1)}, u32[]{:S(2)}, u32[]{:S(2)}) %collective-permute-start.2) | collective-permute-done | bytes 589856 | tf_op jit(solution)/shard_map/ppermute | solution.py:269
  568.1 24.5 %collective-permute-done.3 = bf16[384,768]{1,0:T(8,128)(2,1)S(1)} collective-permute-done((bf16[384,768]{1,0:T(8,128)(2,1)S(1)}, bf16[384,768]{1,0:T(8,128)(2,1)S(1)}, u32[]{:S(2)}, u32[]{:S(2)}) %collective-permute-start.3) | collective-permute-done | bytes 589856 | tf_op jit(solution)/shard_map/ppermute | solution.py:269
  594.2 40.5 %all-reduce = (f32[768]{0:T(1024)}, f32[768]{0:T(1024)}) all-reduce(f32[768]{0:T(1024)} %get-tuple-element.74, f32[768]{0:T(1024)S(1)} %copy-done.40), channel_id=1, replica_groups=mesh['ba'=2,'row'=4,'col'=4] {'ba','row','col'}, use_global_device_ids=true, to_apply=%region_17.18 | all-reduce | flops 1536 | bytes 12288 | tf_op jit(solution)/shard_map/psum | solution.py:282
  639.3 7.5 %all-reduce.7 = (f32[3,192,192]{2,1,0:T(8,128)S(1)}, f32[2,192,512]{2,1,0:T(8,128)S(1)}) all-reduce(bf16[3,192,192]{2,1,0:T(8,128)(2,1)S(1)} %copy.77, bf16[2,192,512]{2,1,0:T(8,128)(2,1)} %reduce-scatter.21.cloned.1.call-done), channel_id=1, replica_groups=mesh['ba'=2,'row'=4,'col'=4] {'ba'}, use_global_device_ids=true, to_apply=%region_6.7 | all-reduce | flops 307200 | bytes 1843200 | tf_op jit(solution)/shard_map/psum | solution.py:252
  (207 shorter events, 116.7 us)
Async XLA Ops:
  7.2 74.6 %all-gather.10.cloned.1.call-start = ((), (), s32[]{:S(2)}) async-start(), calls=%async_computation.10 | async-start | bytes 1966080 | tf_op jit(solution)/shard_map/all_gather | solution.py:209
  9.1 119.6 %all-gather.6.cloned.1.call-start = ((), (), s32[]{:S(2)}) async-start(), calls=%async_computation.8 | async-start | bytes 4423680 | tf_op jit(solution)/shard_map/all_gather | solution.py:205
  64.8 92.2 %all-gather.8.cloned.1.call-start = ((), (), s32[]{:S(2)}) async-start(), calls=%async_computation.9 | async-start | bytes 1474560 | tf_op jit(solution)/shard_map/all_gather | solution.py:177
  81.7 30.7 %copy-start.39 = (s32[1,4]{1,0:T(1,128)S(1)}, s32[1,4]{1,0:T(1,128)}, u32[]{:S(2)}) copy-start(s32[1,4]{1,0:T(1,128)} %param.13) | copy-start | bytes 52
  81.7 136.8 %all-gather.12.cloned.1.call-start = ((), (), s32[]{:S(2)}) async-start(), calls=%async_computation.11 | async-start | bytes 7864320 | tf_op jit(solution)/shard_map/all_gather | solution.py:208
  82.3 181.9 %all-gather.14.cloned.1.call-start = ((), (), s32[]{:S(2)}) async-start(), calls=%async_computation.12 | async-start | bytes 3932160 | tf_op jit(solution)/shard_map/all_gather | solution.py:177
  82.3 34.0 %collective-permute-start = (bf16[384,768]{1,0:T(8,128)(2,1)S(1)}, bf16[384,768]{1,0:T(8,128)(2,1)S(1)}, u32[]{:S(2)}, u32[]{:S(2)}) collective-permute-start(bf16[384,768]{1,0:T(8,128)(2,1)S(1)} %copy-done.10), channel_id=1, source_target_pairs={{0,1},{1,2},{2,3},{4,5},{5,6},{6,7},{8,9},{9,10},{10,11},{12,13},{... | collective-permute-start | bytes 1769480 | tf_op jit(solution)/shard_map/ppermute | solution.py:200
  112.3 245.7 %reduce-scatter.27.cloned.1.call-start = ((), (), s32[]{:S(2)}) async-start(), calls=%async_computation.19 | async-start | bytes 1474560
  116.4 11.4 %collective-permute-start.1 = (bf16[384,768]{1,0:T(8,128)(2,1)S(1)}, bf16[384,768]{1,0:T(8,128)(2,1)S(1)}, u32[]{:S(2)}, u32[]{:S(2)}) collective-permute-start(bf16[384,768]{1,0:T(8,128)(2,1)S(1)} %collective-permute-done), channel_id=1, source_target_pairs={{0,1},{1,2},{2,3},{4,5},{5,6},{6,7},{8,9},{9,10},{10,11},{12,13},{... | collective-permute-start | bytes 1769480 | tf_op jit(solution)/shard_map/ppermute | solution.py:200
  293.0 75.7 %reduce-scatter.29.cloned.1.call-start = ((), (), s32[]{:S(2)}) async-start(), calls=%async_computation.20 | async-start | bytes 3932160
  320.7 71.6 %reduce-scatter.17.cloned.1.call-start = ((), (), s32[]{:S(2)}) async-start(), calls=%async_computation.14 | async-start | bytes 491520 | tf_op jit(solution)/shard_map/reduce_scatter | solution.py:251
  360.6 59.4 %reduce-scatter.23.cloned.1.call-start = ((), (), s32[]{:S(2)}) async-start(), calls=%async_computation.17 | async-start | bytes 1310720 | tf_op jit(solution)/shard_map/reduce_scatter | solution.py:251
  374.0 94.9 %reduce-scatter.15.cloned.1.call-start = ((), (), s32[]{:S(2)}) async-start(), calls=%async_computation.13 | async-start | bytes 4423680 | tf_op jit(solution)/shard_map/reduce_scatter | solution.py:250
  382.8 159.3 %reduce-scatter.19.cloned.1.call-start = ((), (), s32[]{:S(2)}) async-start(), calls=%async_computation.15 | async-start | bytes 7864320 | tf_op jit(solution)/shard_map/reduce_scatter | solution.py:250
  392.2 243.7 %all-reduce.6.cloned.1.call-start = ((), (), s32[]{:S(2)}) async-start(), calls=%async_computation.21 | async-start | bytes 1441792 | tf_op jit(solution)/shard_map/psum | solution.py:252
  421.8 216.0 %reduce-scatter.25.cloned.1.call-start = ((), (), s32[]{:S(2)}) async-start(), calls=%async_computation.18 | async-start | bytes 1228800
  473.7 68.4 %copy-start.22 = (bf16[1152,12,64]{0,2,1:T(8,128)(2,1)S(1)}, bf16[1152,12,64]{0,2,1:T(8,128)(2,1)}, u32[]{:S(2)}) copy-start(bf16[1152,12,64]{0,2,1:T(8,128)(2,1)} %copy-done.21) | copy-start | bytes 5308420
  473.7 165.5 %reduce-scatter.21.cloned.1.call-start = ((), (), s32[]{:S(2)}) async-start(), calls=%async_computation.16 | async-start | bytes 1966080 | tf_op jit(solution)/shard_map/reduce_scatter | solution.py:251
  547.2 17.1 %collective-permute-start.2 = (bf16[384,768]{1,0:T(8,128)(2,1)S(1)}, bf16[384,768]{1,0:T(8,128)(2,1)S(1)}, u32[]{:S(2)}, u32[]{:S(2)}) collective-permute-start(bf16[384,768]{1,0:T(8,128)(2,1)S(1)} %slice.203), channel_id=1, source_target_pairs={{1,0},{2,1},{3,2},{5,4},{6,5},{7,6},{9,8},{10,9},{11,10},{13,12},{... | collective-permute-start | bytes 1769480 | tf_op jit(solution)/shard_map/ppermute | solution.py:269
  564.4 28.2 %collective-permute-start.3 = (bf16[384,768]{1,0:T(8,128)(2,1)S(1)}, bf16[384,768]{1,0:T(8,128)(2,1)S(1)}, u32[]{:S(2)}, u32[]{:S(2)}) collective-permute-start(bf16[384,768]{1,0:T(8,128)(2,1)S(1)} %fusion.25), channel_id=1, source_target_pairs={{1,0},{2,1},{3,2},{5,4},{6,5},{7,6},{9,8},{10,9},{11,10},{13,12},{... | collective-permute-start | bytes 1769480 | tf_op jit(solution)/shard_map/ppermute | solution.py:269
  565.8 26.8 %copy-start.11 = (bf16[384,768]{1,0:T(8,128)(2,1)S(1)}, bf16[384,768]{1,0:T(8,128)(2,1)}, u32[]{:S(2)}) copy-start(bf16[384,768]{1,0:T(8,128)(2,1)} %param.12) | copy-start | bytes 1769476
  565.8 26.8 %copy-start.20 = (bf16[384,12,64]{0,2,1:T(8,128)(2,1)S(1)}, bf16[384,12,64]{0,2,1:T(8,128)(2,1)}, u32[]{:S(2)}) copy-start(bf16[384,12,64]{0,2,1:T(8,128)(2,1)} %maximum_convert_fusion.1) | copy-start | bytes 1769476
  565.8 26.8 %copy-start.38 = (f32[768]{0:T(1024)S(1)}, f32[768]{0:T(1024)}, u32[]{:S(2)}) copy-start(f32[768]{0:T(1024)} %param.21) | copy-start | bytes 9220
  568.1 66.6 %copy-start.6 = (f32[384,768]{1,0:T(8,128)S(1)}, f32[384,768]{1,0:T(8,128)}, u32[]{:S(2)}) copy-start(f32[384,768]{1,0:T(8,128)} %copy-done.5) | copy-start | bytes 3538948
  (41 other events, 275.2 us)
Sparse Core Ops, SparseCore 0:
  10.2 57.8 all-gather.9
  69.9 46.4 all-gather.5
  118.8 27.7 all-gather.7
  148.2 70.1 all-gather.11
  220.2 43.9 all-gather.13
  293.1 28.5 reduce-scatter.26
  324.7 43.9 reduce-scatter.28
  371.5 20.5 reduce-scatter.16
  394.6 25.3 reduce-scatter.22
  422.9 45.8 reduce-scatter.14
  471.8 70.1 reduce-scatter.18
  544.9 19.0 all-reduce.5
  566.5 31.9 reduce-scatter.24
  600.6 34.2 reduce-scatter.20

commit v2 on v1

v2 whole, which is shorter than its diff:
```python
import functools
import jax
import jax.numpy as jnp
from jax import lax
from jax.experimental import pallas as pl
from jax.experimental.pallas import tpu as pltpu
from jax.sharding import PartitionSpec as P

HEAD_DIM = 64
PAIR = 2 * HEAD_DIM
LONGEST = 768
EPSILON = 1e-06
ROPE_BASE = 10000.0
Q_ROWS = 128
NEG = -1e30
SCALE = HEAD_DIM ** (-0.5)
VMEM_LIMIT = 56 * 1024 * 1024
LOW = jnp.bfloat16
F32 = jnp.float32


def contract(left, right, first, second):
    return lax.dot_general(
        left, right, (((first,), (second,)), ((), ())), preferred_element_type=F32
    )


def seq_starts(lengths, places):
    starts = jnp.zeros_like(places)
    end = jnp.int32(0)
    for length in lengths:
        end = end + length
        starts = jnp.where(places >= end, end, starts)
    return starts


def split_heads(pair):
    lane = lax.broadcasted_iota(jnp.int32, pair.shape, 1)
    zero = jnp.zeros_like(pair)
    return jnp.concatenate(
        [jnp.where(lane < HEAD_DIM, pair, zero), jnp.where(lane >= HEAD_DIM, pair, zero)], axis=0
    )


def join_heads(stacked):
    rows = stacked.shape[0] // 2
    lane = lax.broadcasted_iota(jnp.int32, (rows, PAIR), 1)
    return jnp.where(lane < HEAD_DIM, stacked[:rows], stacked[rows:])


def rotate_pair(pair, cosine, sine):
    half = HEAD_DIM // 2
    lane = lax.broadcasted_iota(jnp.int32, pair.shape, 1)
    other = jnp.where(
        lane % HEAD_DIM < half, pltpu.roll(pair, PAIR - half, 1), pltpu.roll(pair, half, 1)
    )
    return pair * cosine + other * sine


class Layout:
    def __init__(self, n_row, n_col, seqs):
        self.n_row, self.n_col, self.seqs = n_row, n_col, seqs

    def lengths(self, info):
        return [info[j] for j in range(self.seqs)]

    def first(self, info):
        return info[self.seqs]

    def core(self, info):
        return info[self.seqs + 1]

    def flip(self, info):
        return info[self.seqs + 2]

    def col(self, info):
        return info[self.seqs + 3]

    def places(self, info, pieces):
        count = self.n_row * self.n_col
        slot = 0
        found = []
        for piece in pieces:
            for index in range(piece.shape[0]):
                core = self.core(info) if slot < count else 1 - self.core(info)
                place = slot % count
                row = jnp.bitwise_xor(jnp.int32(place // self.n_col), self.flip(info))
                step = place % self.n_col
                col = lax.rem(self.col(info) + (self.n_col - step), self.n_col)
                found.append((piece, index, core, row, step, col))
                slot += 1
        return found


def norm_rows(values, gain):
    scale = lax.rsqrt(jnp.mean(values * values, axis=1, keepdims=True) + EPSILON)
    return scale, values * scale * gain


def project_kernel(layout, blocks, *refs):
    info = refs[0]
    seen = refs[1 : 1 + blocks]
    gain_ref, cos_ref, sin_ref = refs[1 + blocks : 4 + blocks]
    n_out = 8
    pieces = refs[4 + blocks : -(n_out + 2)]
    h_ref, q_ref, k_ref, v_ref, wq_ref, wk_ref, wv_ref, wo_ref, buf, sems = refs[-(n_out + 2) :]
    copies = []
    for i, (piece, index, core, row, _, col) in enumerate(layout.places(info, pieces)):
        copy = pltpu.make_async_copy(piece.at[index], buf.at[core, row, col], sems.at[i])
        copy.start()
        copies.append(copy)
    rows = seen[0].shape[0]
    for j, ref in enumerate(seen):
        _, normed = norm_rows(ref[...].astype(F32), gain_ref[...])
        h_ref[j * rows : (j + 1) * rows] = normed.astype(LOW)
    for copy in copies:
        copy.wait()
    deep, wide = buf.shape[3], buf.shape[4] // 2
    outs = ((wq_ref, wk_ref), (wv_ref, wo_ref))
    for core in range(2):
        for row in range(layout.n_row):
            for col in range(layout.n_col):
                for part in range(2):
                    outs[core][part][
                        row * deep : (row + 1) * deep, col * wide : (col + 1) * wide
                    ] = buf[core, row, col, :, part * wide : (part + 1) * wide]
    for j in range(blocks):
        place = slice(j * rows, (j + 1) * rows)
        h = h_ref[place]
        cosine, sine = cos_ref[place], sin_ref[place]
        for pair in range(h.shape[1] // PAIR):
            lanes = slice(pair * PAIR, (pair + 1) * PAIR)
            k_ref[place, lanes] = rotate_pair(
                contract(h, wk_ref[:, lanes], 1, 0), cosine, sine
            ).astype(LOW)
            v_ref[place, lanes] = contract(h, wv_ref[:, lanes], 1, 0).astype(LOW)
            if j == blocks - 1:
                q_ref[:, lanes] = rotate_pair(
                    contract(h, wq_ref[:, lanes], 1, 0), cosine, sine
                ).astype(LOW)


def project(layout, info, blocks, gain, cosine, sine, pieces):
    rows, width = blocks[0].shape
    all_rows = rows * len(blocks)
    deep, lanes = pieces[0].shape[1:]
    n_blocks = 2 * layout.n_row * layout.n_col
    vmem, anyspace = pl.BlockSpec(memory_space=pltpu.VMEM), pl.BlockSpec(memory_space=pl.ANY)
    square = jax.ShapeDtypeStruct((width, width), LOW)
    long = jax.ShapeDtypeStruct((all_rows, width), LOW)
    return pl.pallas_call(
        functools.partial(project_kernel, layout, len(blocks)),
        out_shape=(long, jax.ShapeDtypeStruct((rows, width), LOW), long, long)
        + (square,) * 4,
        in_specs=[pl.BlockSpec(memory_space=pltpu.SMEM)]
        + [vmem] * (len(blocks) + 3)
        + [anyspace] * len(pieces),
        out_specs=(vmem,) * 8,
        scratch_shapes=[
            pltpu.VMEM((2, layout.n_row, layout.n_col, deep, lanes), LOW),
            pltpu.SemaphoreType.DMA((n_blocks,)),
        ],
        compiler_params=pltpu.CompilerParams(vmem_limit_bytes=VMEM_LIMIT),
        cost_estimate=pl.CostEstimate(
            flops=2 * all_rows * width * width * 3, bytes_accessed=20_000_000, transcendentals=0
        ),
        name="project",
    )(info, *blocks, gain, cosine, sine, *pieces)


def attend_forward_kernel(
    layout, info, q_ref, k_ref, v_ref, wo_ref, x_ref, gain_ref, o_ref, mid_ref, h_ref
):
    step = pl.program_id(0)
    halo = k_ref.shape[0] - pl.num_programs(0) * Q_ROWS
    window = halo + Q_ROWS
    first_query = layout.first(info) + step * Q_ROWS
    query_place = first_query + lax.broadcasted_iota(jnp.int32, (Q_ROWS, 1), 0)
    start = seq_starts(layout.lengths(info), query_place)
    key_place = first_query - halo + lax.broadcasted_iota(jnp.int32, (Q_ROWS, window), 1)
    bias = jnp.where((key_place >= start) & (key_place <= query_place), 0.0, NEG)
    bias = jnp.concatenate([bias, bias], axis=0)
    first = pl.multiple_of(step * Q_ROWS, Q_ROWS)
    for pair in range(q_ref.shape[1] // PAIR):
        lanes = slice(pair * PAIR, (pair + 1) * PAIR)
        query = split_heads(q_ref[:, lanes] * SCALE)
        keys = k_ref[pl.ds(first, window), lanes]
        scores = contract(query, keys, 1, 1) + bias
        peak = jnp.max(scores, axis=1, keepdims=True)
        weights = jnp.exp(scores - peak)
        total = jnp.sum(weights, axis=1, keepdims=True)
        out = contract(weights.astype(LOW), v_ref[pl.ds(first, window), lanes], 1, 0)
        o_ref[:, lanes] = join_heads(out / total).astype(o_ref.dtype)
    middle = x_ref[...].astype(F32) + contract(o_ref[...], wo_ref[...], 1, 1)
    mid_ref[...] = middle
    _, normed = norm_rows(middle, gain_ref[...])
    h_ref[...] = normed.astype(LOW)


def attend_forward(layout, info, query, keys, values, w_out_t, tokens, gain):
    rows, width = query.shape

    def whole(array):
        return pl.BlockSpec(array.shape, lambda i: (0, 0))

    part = pl.BlockSpec((Q_ROWS, width), lambda i: (i, 0))
    return pl.pallas_call(
        functools.partial(attend_forward_kernel, layout),
        out_shape=(
            jax.ShapeDtypeStruct(query.shape, LOW),
            jax.ShapeDtypeStruct(query.shape, F32),
            jax.ShapeDtypeStruct(query.shape, LOW),
        ),
        grid=(rows // Q_ROWS,),
        in_specs=[
            pl.BlockSpec(memory_space=pltpu.SMEM), part, whole(keys), whole(values),
            whole(w_out_t), part, whole(gain),
        ],
        out_specs=(part, part, part),
        compiler_params=pltpu.CompilerParams(vmem_limit_bytes=VMEM_LIMIT),
        cost_estimate=pl.CostEstimate(
            flops=8_000_000_000, bytes_accessed=9_000_000, transcendentals=4_000_000
        ),
        name="attend_forward",
    )(info, query, keys, values, w_out_t, tokens, gain)


def mlp_kernel(layout, *refs):
    info, h_ref, mid_ref, dy_ref, gain_ref, wo_ref = refs[:6]
    n_out = 7
    n_scratch = 6
    pieces = refs[6 : -(n_out + n_scratch)]
    out_ref, keep_ref, send_ref, dmid_ref, dm_ref, dheads_ref, dgain_ref = refs[
        -(n_out + n_scratch) : -n_scratch
    ]
    w_in, w_down, acc, acc_back, sems_in, sems_down = refs[-n_scratch:]
    core_here = layout.core(info)
    chunk = w_down.shape[2]
    half = chunk // 2
    deep = pieces[0].shape[1]
    waits = [[] for _ in range(layout.n_col)]
    for i, (piece, index, core, row, step, _) in enumerate(layout.places(info, pieces)):
        place = pl.ds(pl.multiple_of(row * deep, 16), deep)
        copies = (
            pltpu.make_async_copy(
                piece.at[index, :, pl.ds(0, chunk)], w_in.at[core, step, place], sems_in.at[i]
            ),
            pltpu.make_async_copy(
                piece.at[index, :, pl.ds(chunk, half)],
                w_down.at[step, place, pl.ds(pl.multiple_of(core * half, half), half)],
                sems_down.at[i],
            ),
        )
        for copy in copies:
            copy.start()
        waits[step].extend(copies)
    h = h_ref[...]
    dy = dy_ref[...]
    width = keep_ref.shape[1] // 3
    for step in range(layout.n_col):
        for copy in waits[step]:
            copy.wait()
        gate = contract(h, w_in[0, step], 1, 0)
        up = contract(h, w_in[1, step], 1, 0)
        grad = contract(dy, w_down[step], 1, 0)
        sig = jax.nn.sigmoid(gate)
        silu = gate * sig
        hidden = (silu * up).astype(LOW)
        d_gate = (grad * up * (sig + silu * (1.0 - sig))).astype(LOW)
        d_up = (grad * silu).astype(LOW)
        for j, value in enumerate((hidden, d_gate, d_up)):
            lanes = slice(j * width + step * half, j * width + (step + 1) * half)
            keep_ref[:, lanes] = jnp.where(core_here == 0, value[:, :half], value[:, half:])
            send_ref[:, lanes] = jnp.where(core_here == 0, value[:, half:], value[:, :half])
        out = contract(hidden, w_down[step], 1, 1)
        back = contract(d_gate, w_in[0, step], 1, 1) + contract(d_up, w_in[1, step], 1, 1)
        if step == 0:
            acc[...] = out
            acc_back[...] = back
        else:
            acc[...] += out
            acc_back[...] += back
    middle = mid_ref[...]
    out_ref[...] = (middle + acc[...]).astype(LOW)
    d_h = acc_back[...]
    scale = lax.rsqrt(jnp.mean(middle * middle, axis=1, keepdims=True) + EPSILON)
    weighted = d_h * gain_ref[...]
    inner = jnp.mean(weighted * middle, axis=1, keepdims=True)
    d_middle = dy.astype(F32) + scale * weighted - middle * (scale**3 * inner)
    dgain_ref[...] = jnp.sum(d_h * middle * scale, axis=0, keepdims=True)
    dmid_ref[...] = d_middle
    d_low = d_middle.astype(LOW)
    dm_ref[...] = d_low
    dheads_ref[...] = contract(d_low, wo_ref[...], 1, 0).astype(LOW)


def mlp(layout, info, h, middle, dy, gain, w_out_t, pieces):
    rows, width = h.shape
    deep, lanes = pieces[0].shape[1:]
    chunk = lanes * 2 // 3
    units = chunk * layout.n_col
    n_blocks = 2 * layout.n_row * layout.n_col
    vmem, anyspace = pl.BlockSpec(memory_space=pltpu.VMEM), pl.BlockSpec(memory_space=pl.ANY)

    def like(shape, dtype):
        return jax.ShapeDtypeStruct(shape, dtype)

    return pl.pallas_call(
        functools.partial(mlp_kernel, layout),
        out_shape=(
            like((rows, width), LOW),
            like((rows, 3 * units // 2), LOW),
            like((rows, 3 * units // 2), LOW),
            like((rows, width), F32),
            like((rows, width), LOW),
            like((rows, width), LOW),
            like((1, width), F32),
        ),
        in_specs=[pl.BlockSpec(memory_space=pltpu.SMEM)] + [vmem] * 5 + [anyspace] * len(pieces),
        out_specs=(vmem,) * 7,
        scratch_shapes=[
            pltpu.VMEM((2, layout.n_col, width, chunk), LOW),
            pltpu.VMEM((layout.n_col, width, chunk), LOW),
            pltpu.VMEM((rows, width), F32),
            pltpu.VMEM((rows, width), F32),
            pltpu.SemaphoreType.DMA((n_blocks,)),
            pltpu.SemaphoreType.DMA((n_blocks,)),
        ],
        compiler_params=pltpu.CompilerParams(vmem_limit_bytes=VMEM_LIMIT),
        cost_estimate=pl.CostEstimate(
            flops=12 * rows * width * units, bytes_accessed=20_000_000, transcendentals=rows * units
        ),
        name="mlp",
    )(info, h, middle, dy, gain, w_out_t, *pieces)


def mlp_grads_kernel(layout, info, keep_ref, got_ref, h_ref, h2_ref, dy_ref, dy2_ref, g_ref):
    width = keep_ref.shape[1] // 3
    half = width // layout.n_col
    deep = g_ref.shape[2]
    h_t = jnp.concatenate([h_ref[...], h2_ref[...]], axis=0).T
    dy_t = jnp.concatenate([dy_ref[...], dy2_ref[...]], axis=0).T
    for step in range(layout.n_col):
        col = lax.rem(layout.col(info) + (layout.n_col - step), layout.n_col)
        for j, left in enumerate((dy_t, h_t, h_t)):
            lanes = slice(j * width + step * half, j * width + (step + 1) * half)
            right = jnp.concatenate([keep_ref[:, lanes], got_ref[:, lanes]], axis=0)
            grad = contract(left, right, 1, 0).astype(LOW)
            for row in range(layout.n_row):
                g_ref[row, col, :, j * half : (j + 1) * half] = grad[
                    row * deep : (row + 1) * deep
                ]


def mlp_grads(layout, info, keep, got, h, h_other, dy, dy_other):
    rows, width = h.shape
    half = keep.shape[1] // 3 // layout.n_col
    vmem = pl.BlockSpec(memory_space=pltpu.VMEM)
    shape = (layout.n_row, layout.n_col, width // layout.n_row, 3 * half)
    return pl.pallas_call(
        functools.partial(mlp_grads_kernel, layout),
        out_shape=jax.ShapeDtypeStruct(shape, LOW),
        in_specs=[pl.BlockSpec(memory_space=pltpu.SMEM)] + [vmem] * 6,
        out_specs=vmem,
        compiler_params=pltpu.CompilerParams(vmem_limit_bytes=VMEM_LIMIT),
        cost_estimate=pl.CostEstimate(
            flops=4 * rows * width * keep.shape[1], bytes_accessed=12_000_000, transcendentals=0
        ),
        name="mlp_grads",
    )(info, keep, got, h, h_other, dy, dy_other)


def attend_backward_kernel(
    layout, info, q_ref, k_ref, v_ref, g_ref, cos_ref, sin_ref, cosq_ref, sinq_ref,
    wq_ref, wk_ref, wv_ref, dq_ref, dk_ref, dv_ref, dseen_ref, dk_acc, dv_acc, dq_acc,
):
    step = pl.program_id(0)
    steps = pl.num_programs(0)
    halo = k_ref.shape[0] - steps * Q_ROWS
    window = halo + Q_ROWS
    first_query = layout.first(info) + step * Q_ROWS
    query_place = first_query + lax.broadcasted_iota(jnp.int32, (1, Q_ROWS), 1)
    start = seq_starts(layout.lengths(info), query_place)
    key_place = first_query - halo + lax.broadcasted_iota(jnp.int32, (window, Q_ROWS), 0)
    bias = jnp.where((key_place >= start) & (key_place <= query_place), 0.0, NEG)
    bias = jnp.concatenate([bias, bias], axis=1)
    first = pl.multiple_of(step * Q_ROWS, Q_ROWS)

    @pl.when(step == 0)
    def _():
        dk_acc[...] = jnp.zeros_like(dk_acc)
        dv_acc[...] = jnp.zeros_like(dv_acc)

    cosine, sine = cosq_ref[...], -sinq_ref[...]
    for pair in range(q_ref.shape[1] // PAIR):
        lanes = slice(pair * PAIR, (pair + 1) * PAIR)
        query = split_heads(q_ref[:, lanes] * SCALE)
        grad = split_heads(g_ref[:, lanes])
        keys = k_ref[pl.ds(first, window), lanes]
        scores = contract(keys, query, 1, 1) + bias
        weights = jnp.exp(scores - jnp.max(scores, axis=0, keepdims=True))
        probs = weights * (1.0 / jnp.sum(weights, axis=0, keepdims=True))
        grad_probs = contract(v_ref[pl.ds(first, window), lanes], grad, 1, 1)
        inner = jnp.sum(probs * grad_probs, axis=0, keepdims=True)
        grad_raw = (probs * (grad_probs - inner)).astype(LOW)
        dv_acc[pl.ds(first, window), lanes] += contract(probs.astype(LOW), grad, 1, 0)
        dk_acc[pl.ds(first, window), lanes] += contract(grad_raw, query, 1, 0)
        grad_query = join_heads(contract(grad_raw, keys, 0, 0)) * SCALE
        dq = rotate_pair(grad_query, cosine, sine).astype(LOW)
        dq_ref[:, lanes] = dq
        dq_acc[pl.ds(first, Q_ROWS), lanes] = dq

    @pl.when(step == steps - 1)
    def _():
        rows = dq_acc.shape[0]
        blocks = dk_acc.shape[0] // rows
        for j in range(blocks):
            place = slice(j * rows, (j + 1) * rows)
            for pair in range(q_ref.shape[1] // PAIR):
                lanes = slice(pair * PAIR, (pair + 1) * PAIR)
                dk_ref[place, lanes] = rotate_pair(
                    dk_acc[place, lanes], cos_ref[place], -sin_ref[place]
                ).astype(LOW)
                dv_ref[place, lanes] = dv_acc[place, lanes].astype(LOW)
            seen = contract(dk_ref[place], wk_ref[...], 1, 1)
            seen = seen + contract(dv_ref[place], wv_ref[...], 1, 1)
            if j == blocks - 1:
                seen = seen + contract(dq_acc[...], wq_ref[...], 1, 1)
            dseen_ref[place] = seen


def attend_backward(layout, info, query, keys, values, grads, cosine, sine, w_q, w_k, w_v):
    rows, width = query.shape
    halo_steps = (keys.shape[0] - rows) // Q_ROWS

    def whole(array):
        return pl.BlockSpec(array.shape, lambda i: (0, 0))

    part = pl.BlockSpec((Q_ROWS, width), lambda i: (i, 0))
    own = pl.BlockSpec((Q_ROWS, PAIR), lambda i: (halo_steps + i, 0))
    return pl.pallas_call(
        functools.partial(attend_backward_kernel, layout),
        out_shape=(
            jax.ShapeDtypeStruct(query.shape, LOW),
            jax.ShapeDtypeStruct(keys.shape, LOW),
            jax.ShapeDtypeStruct(keys.shape, LOW),
            jax.ShapeDtypeStruct(keys.shape, F32),
        ),
        grid=(rows // Q_ROWS,),
        in_specs=[
            pl.BlockSpec(memory_space=pltpu.SMEM), part, whole(keys), whole(values), part,
            whole(cosine), whole(sine), own, own, whole(w_q), whole(w_k), whole(w_v),
        ],
        out_specs=(part, whole(keys), whole(keys), whole(keys)),
        scratch_shapes=[
            pltpu.VMEM(keys.shape, F32),
            pltpu.VMEM(keys.shape, F32),
            pltpu.VMEM(query.shape, LOW),
        ],
        compiler_params=pltpu.CompilerParams(vmem_limit_bytes=VMEM_LIMIT),
        cost_estimate=pl.CostEstimate(
            flops=25_000_000_000, bytes_accessed=20_000_000, transcendentals=4_000_000
        ),
        name="attend_backward",
    )(info, query, keys, values, grads, cosine, sine, cosine, sine, w_q, w_k, w_v)


def attend_grads_kernel(
    layout, info, h_ref, dq_ref, dk_ref, dv_ref, heads_ref, dm_ref, keep_ref, send_ref
):
    rows = dq_ref.shape[0]
    halo = h_ref.shape[0] - rows
    deep = keep_ref.shape[2]
    wide = keep_ref.shape[3] // 2
    h_t = h_ref[...].T
    dm_t = dm_ref[...].T
    grads = (
        contract(h_t[:, halo:], dq_ref[...], 1, 0).astype(LOW),
        contract(h_t, dk_ref[...], 1, 0).astype(LOW),
        contract(h_t, dv_ref[...], 1, 0).astype(LOW),
        contract(dm_t, heads_ref[...], 1, 0).astype(LOW),
    )
    for core, (kept, sent) in enumerate(((keep_ref, send_ref), (send_ref, keep_ref))):

        @pl.when(layout.core(info) == core)
        def _(kept=kept, sent=sent):
            for j, ref in enumerate((kept, kept, sent, sent)):
                for row in range(layout.n_row):
                    place = jnp.bitwise_xor(jnp.int32(row), layout.flip(info))
                    for col in range(layout.n_col):
                        step = lax.rem(layout.col(info) + (layout.n_col - col), layout.n_col)
                        part = j % 2
                        ref[place, step, :, part * wide : (part + 1) * wide] = grads[j][
                            row * deep : (row + 1) * deep, col * wide : (col + 1) * wide
                        ]


def attend_grads(layout, info, h, dq, dk, dv, heads, dm):
    rows, width = dq.shape
    vmem = pl.BlockSpec(memory_space=pltpu.VMEM)
    shape = (layout.n_row, layout.n_col, width // layout.n_row, 2 * width // layout.n_col)
    return pl.pallas_call(
        functools.partial(attend_grads_kernel, layout),
        out_shape=(jax.ShapeDtypeStruct(shape, LOW),) * 2,
        in_specs=[pl.BlockSpec(memory_space=pltpu.SMEM)] + [vmem] * 6,
        out_specs=(vmem, vmem),
        compiler_params=pltpu.CompilerParams(vmem_limit_bytes=VMEM_LIMIT),
        cost_estimate=pl.CostEstimate(
            flops=16 * rows * width * width, bytes_accessed=12_000_000, transcendentals=0
        ),
        name="attend_grads",
    )(info, h, dq, dk, dv, heads, dm)


def shift(count, by):
    return [(i, (i + by) % count) for i in range(count)]


SWAP = [(0, 1), (1, 0)]


def gather(layout, block):
    n_row, n_col = layout.n_row, layout.n_col
    plane = jnp.stack(
        [block] + [lax.ppermute(block, "col", shift(n_col, k)) for k in range(1, n_col)]
    )
    if n_row == 4:
        along_x = [(i, i ^ 1) for i in range(4)]
        along_y = [(i, i ^ 2) for i in range(4)]
        from_x = lax.ppermute(plane, "row", along_x)
        from_y = lax.ppermute(plane, "row", along_y)
        cut = n_col // 2
        diagonal = (
            lax.ppermute(from_x[:cut], "row", along_y),
            lax.ppermute(from_y[cut:], "row", along_x),
        )
        pieces = [plane, from_x, from_y, *diagonal]
    else:
        pieces = [lax.all_gather(plane, "row", axis=0, tiled=True)]
    return pieces + [lax.ppermute(piece, "ba", SWAP) for piece in pieces]


def plus(left, right):
    return left.astype(F32) + right.astype(F32)


def scatter(layout, grads):
    n_row, n_col = layout.n_row, layout.n_col
    if n_row == 4:
        along_x = [(i, i ^ 1) for i in range(4)]
        along_y = [(i, i ^ 2) for i in range(4)]
        cut = n_col // 2
        got_x = lax.ppermute(
            jnp.stack([grads[1, :cut], grads[3, :cut]]), "row", along_x
        )
        got_y = lax.ppermute(
            jnp.stack([grads[2, cut:], grads[3, cut:]]), "row", along_y
        )
        on_y = lax.ppermute(plus(grads[2, :cut], got_x[1]).astype(LOW), "row", along_y)
        on_x = lax.ppermute(plus(grads[1, cut:], got_y[1]).astype(LOW), "row", along_x)
        plane = jnp.concatenate(
            [
                plus(grads[0, :cut], got_x[0]) + on_y.astype(F32),
                plus(grads[0, cut:], got_y[0]) + on_x.astype(F32),
            ]
        ).astype(LOW)
    else:
        plane = lax.psum_scatter(grads, "row", scatter_dimension=0, tiled=True)[0]
    total = plane[0].astype(F32)
    for k in range(1, n_col):
        total = total + lax.ppermute(plane[k], "col", shift(n_col, n_col - k)).astype(F32)
    return total


def shards(
    n_row, n_col, tokens, lengths, w_query, w_key, w_value, w_out, w_gate, w_up, w_down,
    gain_attn, gain_mlp, cotangent,
):
    rows, width = tokens.shape
    core, row, col = lax.axis_index("ba"), lax.axis_index("row"), lax.axis_index("col")
    layout = Layout(n_row, n_col, lengths.shape[1])
    hops = -(-(LONGEST - 1) // rows)
    halo = hops * rows
    step_right = [(i, i + 1) for i in range(n_col - 1)]
    step_left = [(i + 1, i) for i in range(n_col - 1)]

    first_core = core == 0
    half_units = w_down.shape[0] // 2
    w_down_t = w_down.T
    attn_block = jnp.where(
        first_core,
        jnp.concatenate([w_query, w_key], axis=1),
        jnp.concatenate([w_value, w_out.T], axis=1),
    )
    mlp_block = jnp.where(
        first_core,
        jnp.concatenate([w_gate, w_down_t[:, :half_units]], axis=1),
        jnp.concatenate([w_up, w_down_t[:, half_units:]], axis=1),
    )
    attn_pieces = gather(layout, attn_block)
    blocks = [tokens]
    for _ in range(hops):
        blocks.insert(0, lax.ppermute(blocks[0], "col", step_right))
    mlp_pieces = gather(layout, mlp_block)
    dy_other = lax.ppermute(cotangent, "ba", SWAP)

    first = col * rows
    flip = row if n_row == 4 else jnp.int32(0)
    info = jnp.concatenate([lengths[0], jnp.stack([first, core, flip, col])]).astype(jnp.int32)
    place = first - halo + jnp.arange(halo + rows, dtype=jnp.int32)
    seq_list = [lengths[0, j] for j in range(lengths.shape[1])]
    position = (place - seq_starts(seq_list, place)).astype(F32)
    half = HEAD_DIM // 2
    lane = jnp.arange(PAIR)
    frequency = ROPE_BASE ** (-(lane % half).astype(F32) / half)
    angles = position[:, None] * frequency[None, :]
    cosine = jnp.cos(angles)
    sine = jnp.sin(angles) * jnp.where(lane % HEAD_DIM < half, -1.0, 1.0)[None, :]

    h1, q, k, v, w_q, w_k, w_v, w_o_t = project(
        layout, info, blocks, gain_attn[None], cosine, sine, attn_pieces
    )
    heads, middle, h2 = attend_forward(
        layout, info, q, k, v, w_o_t, tokens, gain_mlp[None]
    )
    h2_other = lax.ppermute(h2, "ba", SWAP)
    layer_out, keep, send, d_middle, dm, d_heads, dgain_mlp = mlp(
        layout, info, h2, middle, cotangent, gain_mlp[None], w_o_t, mlp_pieces
    )
    got = lax.ppermute(send, "ba", SWAP)
    grads_mlp = mlp_grads(layout, info, keep, got, h2, h2_other, cotangent, dy_other)
    part = lax.psum_scatter(grads_mlp, "row", scatter_dimension=0, tiled=True)
    part = lax.psum_scatter(part, "col", scatter_dimension=1, tiled=True)[0, 0]

    dq, dk, dv, d_seen = attend_backward(
        layout, info, q, k, v, d_heads, cosine, sine, w_q, w_k, w_v
    )
    keep_attn, send_attn = attend_grads(layout, info, h1, dq, dk, dv, heads, dm)
    got_attn = lax.ppermute(send_attn, "ba", SWAP)
    part_attn = scatter(layout, plus(keep_attn, got_attn).astype(LOW))

    d_h1 = d_seen[halo:]
    travelling = d_seen[:rows].astype(LOW)
    for hop in range(hops):
        arrived = lax.ppermute(travelling, "col", step_left).astype(F32)
        if hop + 1 < hops:
            travelling = (d_seen[(hop + 1) * rows : (hop + 2) * rows] + arrived).astype(LOW)
        else:
            d_h1 = d_h1 + arrived
    x = tokens.astype(F32)
    scale = lax.rsqrt(jnp.mean(x * x, axis=1, keepdims=True) + EPSILON)
    weighted = d_h1 * gain_attn[None, :]
    inner = jnp.mean(weighted * x, axis=1, keepdims=True)
    input_grad = (d_middle + scale * weighted - x * (scale**3 * inner)).astype(LOW)
    dgain_attn = jnp.sum(d_h1 * x * scale, axis=0)

    other_attn = lax.ppermute(part_attn, "ba", SWAP)
    lower = jnp.where(first_core, part_attn, other_attn)
    upper = jnp.where(first_core, other_attn, part_attn)
    wide = width // n_col
    part = part.astype(F32)
    other = lax.ppermute(part, "ba", SWAP)
    cut = part.shape[1] // 3

    def whole(j):
        mine, theirs = part[:, j * cut : (j + 1) * cut], other[:, j * cut : (j + 1) * cut]
        return jnp.concatenate(
            [jnp.where(first_core, mine, theirs), jnp.where(first_core, theirs, mine)], axis=1
        )

    grad_gain_attn, grad_gain_mlp = lax.psum((dgain_attn, dgain_mlp[0]), ("ba", "row", "col"))
    return (
        layer_out, input_grad, lower[:, :wide], lower[:, wide:], upper[:, :wide],
        upper[:, wide:].T, whole(1), whole(2), whole(0).T, grad_gain_attn, grad_gain_mlp,
    )


def solution(mesh):
    tokens = P(("ba", "row", "col"), None)
    in_side, out_side = P("row", "col"), P("col", "row")
    in_specs = (
        tokens, P(("ba", "row"), None), in_side, in_side, in_side, out_side, in_side, in_side,
        out_side, P(), P(), tokens,
    )
    out_specs = (
        tokens, tokens, in_side, in_side, in_side, out_side, in_side, in_side, out_side, P(), P(),
    )
    body = functools.partial(shards, mesh.shape["row"], mesh.shape["col"])
    return jax.shard_map(
        body, mesh=mesh, in_specs=in_specs, out_specs=out_specs, check_vma=False
    )
```

time: 667 us -> 356 us (0.53); the launches traced: 656 us -> 352 us
  waiting for transfers between devices: 288 us -> 98.8 us
  blocking collectives: 143 us -> 40.5 us
  Pallas kernels: 35.6 us -> 99 us
  matrix products: 62.6 us -> 0 us
  local copies, waits for them, and re-layouts: 75.1 us -> 13.5 us
  starting transfers between devices: 10.8 us -> 61.2 us
    reduce_scatter x5 -> x1, waiting for transfers between devices: 141 us -> 0.01 us  [shards(): part = lax.psum_scatter(part, 'col', scatter_dimension=1, tiled=True)[0, 0]]
    all_gather x3 -> x0, blocking collectives: 95.2 us -> none  [the longest x1 52.3 us: shards(): lax.all_gather(w_qkv, 'col', axis=2, tiled=True)]
    all_gather x5 -> x0, waiting for transfers between devices: 94.1 us -> none  [the longest x1 56.8 us: shards(): lax.all_gather(lax.all_gather(jnp.stack([w_gate, w_up]), 'col', axis=2, t...]
    pallas_call x2 -> x6, Pallas kernels: 35.6 us -> 99 us  [the longest x1 32.7 us: attend_backward(): pl.pallas_call(functools.partial(attend_backward_kernel, layout), out_sha...]
    dot_general x21 -> x0, matrix products: 62.6 us -> none  [contract(): lax.dot_general(left, right, (((first,), (second,)), ((), ())), preferred...]
    ppermute x2 -> x39, waiting for transfers between devices: 40.2 us -> 94.2 us  [the longest x2 29.7 us: shards(): arrived = lax.ppermute(travelling, 'col', step_left).astype(F32)]
    unnamed x108 -> x52, local copies, waits for them, and re-layouts: 54.9 us -> 4.5 us
    ppermute x2 -> x39, starting transfers between devices: 2.72 us -> 41.9 us  [the longest x6 10.2 us: gather(): lax.ppermute(block, 'col', shift(n_col, k))]
  transfers between devices with their start and end apart: 18 -> 43, of which waited for: 9 -> 16; matrix products, arithmetic and copies ran while one was open for 19% -> 8% of each run, Pallas kernels for 5% -> 20%
where the time goes in v2:
time: 356 us; the launch traced here: 352 us
  Pallas kernels  99 us (28%)
  waiting for transfers between devices  98.8 us (28%)
  starting transfers between devices  61.2 us (17%)
  blocking collectives  40.5 us (11%)
  other arithmetic  22 us (6%)
  between operations  17.4 us (5%)
  local copies, waits for them, and re-layouts  13.5 us (4%)
    psum x1, blocking collectives, shards(): lax.psum((dgain_attn, dgain_mlp[0]), ('ba', 'row', 'col'))  40.5 us
    pallas_call x1, Pallas kernels, attend_backward(): pl.pallas_call(functools.partial(attend_backward_kernel, layout), out_sha...  32.7 us
    ppermute x2, waiting for transfers between devices, shards(): arrived = lax.ppermute(travelling, 'col', step_left).astype(F32)  29.7 us
    ppermute x2, waiting for transfers between devices, gather(): from_y = lax.ppermute(plane, 'row', along_y)  27.7 us
    ppermute x2, starting transfers between devices, shards(): blocks.insert(0, lax.ppermute(blocks[0], 'col', step_right))  19.2 us
    ppermute x6, waiting for transfers between devices, gather(): lax.ppermute(block, 'col', shift(n_col, k))  19.1 us
    pallas_call x1, Pallas kernels, mlp(): pl.pallas_call(functools.partial(mlp_kernel, layout), out_shape=(like((ro...  17.7 us
    pallas_call x1, Pallas kernels, attend_forward(): pl.pallas_call(functools.partial(attend_forward_kernel, layout), out_shap...  15.1 us
  transfers between devices with their start and end apart: 43, of which 16 were waited for; matrix products, arithmetic and copies ran while one was open for 8% of the time, Pallas kernels for 20%

profile of v2, /device:TPU:0, one launch (start us, length us, event | category | flops | bytes accessed | tf_op | source)
XLA Modules:
  0.0 352.3 jit_solution(12431489469189735018)
XLA Ops:
  9.6 3.1 collective-permute-start.2
  12.6 2.6 collective-permute-start.3
  21.7 4.1 %collective-permute-done.3 = bf16[192,384]{1,0:T(8,128)(2,1)S(1)} collective-permute-done((bf16[192,384]{1,0:T(8,128)(2,1)S(1)}, bf16[192,384]{1,0:T(8,128)(2,1)S(1)}, u32[]{:S(2)}, u32[]{:S(2)}) %collective-permute-start.3) | collective-permute-done | bytes 147488 | tf_op jit(solution)/shard_map/ppermute | solution.py:525
  25.8 5.5 %collective-permute-done.4 = bf16[192,384]{1,0:T(8,128)(2,1)S(1)} collective-permute-done((bf16[192,384]{1,0:T(8,128)(2,1)S(1)}, bf16[192,384]{1,0:T(8,128)(2,1)S(1)}, u32[]{:S(2)}, u32[]{:S(2)}) %collective-permute-start.4) | collective-permute-done | bytes 147488 | tf_op jit(solution)/shard_map/ppermute | solution.py:525
  31.4 6.9 %collective-permute-start.5 = (bf16[4,192,384]{2,1,0:T(8,128)(2,1)S(1)}, bf16[4,192,384]{2,1,0:T(8,128)(2,1)}, u32[]{:S(2)}, u32[]{:S(2)}) collective-permute-start(bf16[4,192,384]{2,1,0:T(8,128)(2,1)S(1)} %pad_maximum_fusion.1.refs_7_), channel_id=1, source_target_pairs={{0,4},{4,0},{8,12},{12,8},{1,5},{5,1},{9,13},{13,9},{2,6},{6,2},{1... | collective-permute-start | bytes 1769480 | tf_op jit(solution)/shard_map/ppermute | solution.py:530
  38.4 8.7 %collective-permute-done.15 = bf16[192,768]{1,0:T(8,128)(2,1)S(1)} collective-permute-done((bf16[192,768]{1,0:T(8,128)(2,1)S(1)}, bf16[192,768]{1,0:T(8,128)(2,1)S(1)}, u32[]{:S(2)}, u32[]{:S(2)}) %collective-permute-start.15) | collective-permute-done | bytes 294944 | tf_op jit(solution)/shard_map/ppermute | solution.py:525
  50.8 9.5 %collective-permute-start = (bf16[384,768]{1,0:T(8,128)(2,1)S(1)}, bf16[384,768]{1,0:T(8,128)(2,1)}, u32[]{:S(2)}, u32[]{:S(2)}) collective-permute-start(bf16[384,768]{1,0:T(8,128)(2,1)S(1)} %copy-done), channel_id=1, source_target_pairs={{0,1},{1,2},{2,3},{4,5},{5,6},{6,7},{8,9},{9,10},{10,11},{12,13},{... | collective-permute-start | bytes 1769480 | tf_op jit(solution)/shard_map/ppermute | solution.py:603
  61.4 27.7 %collective-permute-done.6.refs_9_ = bf16[4,192,384]{2,1,0:T(8,128)(2,1)} collective-permute-done((bf16[4,192,384]{2,1,0:T(8,128)(2,1)S(1)}, bf16[4,192,384]{2,1,0:T(8,128)(2,1)}, u32[]{:S(2)}, u32[]{:S(2)}) %collective-permute-start.6) | collective-permute-done | bytes 589856 | tf_op jit(solution)/shard_map/ppermute | solution.py:531
  92.2 9.7 %collective-permute-start.1 = (bf16[384,768]{1,0:T(8,128)(2,1)}, bf16[384,768]{1,0:T(8,128)(2,1)}, u32[]{:S(2)}, u32[]{:S(2)}) collective-permute-start(bf16[384,768]{1,0:T(8,128)(2,1)} %collective-permute-done.refs_2_), channel_id=1, source_target_pairs={{0,1},{1,2},{2,3},{4,5},{5,6},{6,7},{8,9},{9,10},{10,11},{12,13},{... | collective-permute-start | bytes 1769480 | tf_op jit(solution)/shard_map/ppermute | solution.py:603
  108.0 4.5 %collective-permute-done.1.refs_1_ = bf16[384,768]{1,0:T(8,128)(2,1)} collective-permute-done((bf16[384,768]{1,0:T(8,128)(2,1)}, bf16[384,768]{1,0:T(8,128)(2,1)}, u32[]{:S(2)}, u32[]{:S(2)}) %collective-permute-start.1) | collective-permute-done | bytes 589856 | tf_op jit(solution)/shard_map/ppermute | solution.py:603
  115.2 3.4 fusion.6
  120.3 13.5 %project.1 = (bf16[1152,768]{1,0:T(8,128)(2,1)}, bf16[384,768]{1,0:T(8,128)(2,1)}, bf16[1152,768]{1,0:T(8,128)(2,1)}, bf16[1152,768]{1,0:T(8,128)(2,1)}, bf16[76...) custom-call(s32[8]{0:T(128)} %concatenate.78.refs_0_.info, ...), custom_call_target="tpu_custom_call" | custom-call | flops 4076863488 | bytes 20000000 | tf_op jit(solution)/shard_map/project/pallas_call | solution.py:151
  134.5 15.1 %attend_forward.1 = (bf16[384,768]{1,0:T(8,128)(2,1)}, f32[384,768]{1,0:T(8,128)}, bf16[384,768]{1,0:T(8,128)(2,1)}) custom-call(s32[8]{0:T(128)} %concatenate.78.refs_0_.info, bf16[384,768]{1,0:T(8,128)(2,1)} %get-tuple-element.35.q_ref, bf16[1152,768]{1,0:T(8,128)(2,1)} %get-tuple-element.36.k_ref, bf16[1152,768]{1,0:T(8,128)(2,1)} %get-tuple-element.37.v_ref, ...), custom_call_target="tpu_custom_call" | custom-call | flops 8000000000 | bytes 9000000 | tf_op jit(solution)/shard_map/attend_forward/pallas_call | solution.py:207
  150.6 17.7 %mlp.1 = (bf16[384,768]{1,0:T(8,128)(2,1)}, bf16[384,3072]{1,0:T(8,128)(2,1)}, bf16[384,3072]{1,0:T(8,128)(2,1)}, f32[384,768]{1,0:T(8,128)}, bf16[384,768]{1,0:...) custom-call(s32[8]{0:T(128)} %concatenate.78.refs_0_.info, bf16[384,768]{1,0:T(8,128)(2,1)} %get-tuple-element.39.refs_1_.h_ref, ...), custom_call_target="tpu_custom_call" | custom-call | flops 7247757312 | bytes 20000000 | tf_op jit(solution)/shard_map/mlp/pallas_call | solution.py:308
  169.0 4.5 %collective-permute-done.39.dy2_ref = bf16[384,768]{1,0:T(8,128)(2,1)S(1)} collective-permute-done((bf16[384,768]{1,0:T(8,128)(2,1)S(1)}, bf16[384,768]{1,0:T(8,128)(2,1)S(1)}, u32[]{:S(2)}, u32[]{:S(2)}) %collective-permute-start.39) | collective-permute-done | bytes 589856 | tf_op jit(solution)/shard_map/ppermute | solution.py:605
  176.3 9.0 %mlp_grads.1 = bf16[4,4,192,768]{3,2,1,0:T(8,128)(2,1)} custom-call(s32[8]{0:T(128)} %concatenate.78.refs_0_.info, bf16[384,3072]{1,0:T(8,128)(2,1)} %get-tuple-element.56.keep_ref, bf16[384,3072]{1,0:T(8,128)(2,1)} %copy-done.17, bf16[384,768]{1,0:T(8,128)(2,1)} %get-tuple-element.39.refs_1_.h_ref, bf16[384,768]{1,0:T(8,128)(2,1)} %copy-done.24, ...), custom_call_target="tpu_custom_call" | custom-call | flops 3623878656 | bytes 12000000 | tf_op jit(solution)/shard_map/mlp_grads/pallas_call | solution.py:360
  185.4 32.7 %attend_backward.1 = (bf16[384,768]{1,0:T(8,128)(2,1)}, bf16[1152,768]{1,0:T(8,128)(2,1)}, bf16[1152,768]{1,0:T(8,128)(2,1)}, f32[1152,768]{1,0:T(8,128)}) custom-call(s32[8]{0:T(128)} %concatenate.78.refs_0_.info, bf16[384,768]{1,0:T(8,128)(2,1)} %get-tuple-element.35.q_ref, bf16[1152,768]{1,0:T(8,128)(2,1)} %get-tuple-element.36.k_ref, ...), custom_call_target="tpu_custom_call" | custom-call | flops 24999999488 | bytes 20000000 | tf_op jit(solution)/shard_map/attend_backward/pallas_call | solution.py:441
  218.1 10.9 %attend_grads.1 = (bf16[4,4,192,384]{3,2,1,0:T(8,128)(2,1)}, bf16[4,4,192,384]{3,2,1,0:T(8,128)(2,1)}) custom-call(s32[8]{0:T(128)} %concatenate.78.refs_0_.info, bf16[1152,768]{1,0:T(8,128)(2,1)} %get-tuple-element.48.h_ref, bf16[384,768]{1,0:T(8,128)(2,1)} %get-tuple-element.49.dq_ref, bf16[1152,768]{1,0:T(8,128)(2,1)} %get-tuple-element.50.dk_ref, ...), custom_call_target="tpu_custom_call" | custom-call | flops 3623878656 | bytes 12000000 | tf_op jit(solution)/shard_map/attend_grads/pallas_call | solution.py:502
  230.5 3.3 collective-permute-done.28
  240.1 7.4 %collective-permute-done.26 = bf16[384,768]{1,0:T(8,128)(2,1)S(1)} collective-permute-done((bf16[384,768]{1,0:T(8,128)(2,1)S(1)}, bf16[384,768]{1,0:T(8,128)(2,1)S(1)}, u32[]{:S(2)}, u32[]{:S(2)}) %collective-permute-start.26) | collective-permute-done | bytes 589856 | tf_op jit(solution)/shard_map/ppermute | solution.py:645
  250.1 3.6 %collective-permute-done.29 = bf16[2,2,192,384]{3,2,1,0:T(8,128)(2,1)} collective-permute-done((bf16[2,2,192,384]{3,2,1,0:T(8,128)(2,1)}, bf16[2,2,192,384]{3,2,1,0:T(8,128)(2,1)}, u32[]{:S(2)}, u32[]{:S(2)}) %collective-permute-start.29) | collective-permute-done | bytes 589856 | tf_op jit(solution)/shard_map/ppermute | solution.py:553
  259.6 22.3 %collective-permute-done.27 = bf16[384,768]{1,0:T(8,128)(2,1)S(1)} collective-permute-done((bf16[384,768]{1,0:T(8,128)(2,1)}, bf16[384,768]{1,0:T(8,128)(2,1)S(1)}, u32[]{:S(2)}, u32[]{:S(2)}) %collective-permute-start.27) | collective-permute-done | bytes 589856 | tf_op jit(solution)/shard_map/ppermute | solution.py:645
  293.0 3.2 collective-permute-done.35
  298.8 40.5 %all-reduce.1 = (f32[768]{0:T(1024)}, f32[768]{0:T(1024)}) all-reduce(f32[768]{0:T(1024)S(1)} %get-tuple-element.81, f32[768]{0:T(1024)S(1)} %copy-done.13), channel_id=1, replica_groups=mesh['ba'=2,'row'=4,'col'=4] {'ba','row','col'}, use_global_device_ids=true, to_apply=%region_5.6 | all-reduce | flops 1536 | bytes 12288 | tf_op jit(solution)/shard_map/psum | solution.py:671
  (166 shorter events, 65.5 us)
Async XLA Ops:
  7.2 242.6 %reduce-scatter.7.cloned.1.call-start = ((), (), s32[]{:S(2)}) async-start(), calls=%async_computation.3 | async-start | bytes 5898240
  15.2 16.1 %collective-permute-start.4 = (bf16[192,384]{1,0:T(8,128)(2,1)S(1)}, bf16[192,384]{1,0:T(8,128)(2,1)S(1)}, u32[]{:S(2)}, u32[]{:S(2)}) collective-permute-start(bf16[192,384]{1,0:T(8,128)(2,1)S(1)} %maximum_select_fusion.3), channel_id=1, source_target_pairs={{0,3},{1,0},{2,1},{3,2},{4,7},{5,4},{6,5},{7,6},{8,11},{9,8},{10,9... | collective-permute-start | bytes 442376 | tf_op jit(solution)/shard_map/ppermute | solution.py:525
  17.6 20.7 %collective-permute-start.14 = (bf16[192,768]{1,0:T(8,128)(2,1)S(1)}, bf16[192,768]{1,0:T(8,128)(2,1)S(1)}, u32[]{:S(2)}, u32[]{:S(2)}) collective-permute-start(bf16[192,768]{1,0:T(8,128)(2,1)S(1)} %maximum_select_fusion.1), channel_id=1, source_target_pairs={{0,1},{1,2},{2,3},{3,0},{4,5},{5,6},{6,7},{7,4},{8,9},{9,10},{10,1... | collective-permute-start | bytes 884744 | tf_op jit(solution)/shard_map/ppermute | solution.py:525
  18.4 28.7 %collective-permute-start.15 = (bf16[192,768]{1,0:T(8,128)(2,1)S(1)}, bf16[192,768]{1,0:T(8,128)(2,1)S(1)}, u32[]{:S(2)}, u32[]{:S(2)}) collective-permute-start(bf16[192,768]{1,0:T(8,128)(2,1)S(1)} %maximum_select_fusion.1), channel_id=1, source_target_pairs={{0,2},{1,3},{2,0},{3,1},{4,6},{5,7},{6,4},{7,5},{8,10},{9,11},{10,... | collective-permute-start | bytes 884744 | tf_op jit(solution)/shard_map/ppermute | solution.py:525
  19.4 27.7 %collective-permute-start.16 = (bf16[192,768]{1,0:T(8,128)(2,1)S(1)}, bf16[192,768]{1,0:T(8,128)(2,1)S(1)}, u32[]{:S(2)}, u32[]{:S(2)}) collective-permute-start(bf16[192,768]{1,0:T(8,128)(2,1)S(1)} %maximum_select_fusion.1), channel_id=1, source_target_pairs={{0,3},{1,0},{2,1},{3,2},{4,7},{5,4},{6,5},{7,6},{8,11},{9,8},{10,9... | collective-permute-start | bytes 884744 | tf_op jit(solution)/shard_map/ppermute | solution.py:525
  31.4 28.9 %collective-permute-start.5 = (bf16[4,192,384]{2,1,0:T(8,128)(2,1)S(1)}, bf16[4,192,384]{2,1,0:T(8,128)(2,1)}, u32[]{:S(2)}, u32[]{:S(2)}) collective-permute-start(bf16[4,192,384]{2,1,0:T(8,128)(2,1)S(1)} %pad_maximum_fusion.1.refs_7_), channel_id=1, source_target_pairs={{0,4},{4,0},{8,12},{12,8},{1,5},{5,1},{9,13},{13,9},{2,6},{6,2},{1... | collective-permute-start | bytes 1769480 | tf_op jit(solution)/shard_map/ppermute | solution.py:530
  47.3 55.2 %collective-permute-start.17 = (bf16[4,192,768]{2,1,0:T(8,128)(2,1)S(1)}, bf16[4,192,768]{2,1,0:T(8,128)(2,1)S(1)}, u32[]{:S(2)}, u32[]{:S(2)}) collective-permute-start(bf16[4,192,768]{2,1,0:T(8,128)(2,1)S(1)} %pad_maximum_fusion.refs_6_), channel_id=1, source_target_pairs={{0,4},{4,0},{8,12},{12,8},{1,5},{5,1},{9,13},{13,9},{2,6},{6,2},{1... | collective-permute-start | bytes 3538952 | tf_op jit(solution)/shard_map/ppermute | solution.py:530
  48.8 53.7 %collective-permute-start.18 = (bf16[4,192,768]{2,1,0:T(8,128)(2,1)S(1)}, bf16[4,192,768]{2,1,0:T(8,128)(2,1)}, u32[]{:S(2)}, u32[]{:S(2)}) collective-permute-start(bf16[4,192,768]{2,1,0:T(8,128)(2,1)S(1)} %pad_maximum_fusion.refs_6_), channel_id=1, source_target_pairs={{0,8},{4,12},{8,0},{12,4},{1,9},{5,13},{9,1},{13,5},{2,10},{6,14},... | collective-permute-start | bytes 3538952 | tf_op jit(solution)/shard_map/ppermute | solution.py:531
  50.3 38.7 %collective-permute-start.6 = (bf16[4,192,384]{2,1,0:T(8,128)(2,1)S(1)}, bf16[4,192,384]{2,1,0:T(8,128)(2,1)}, u32[]{:S(2)}, u32[]{:S(2)}) collective-permute-start(bf16[4,192,384]{2,1,0:T(8,128)(2,1)S(1)} %pad_maximum_fusion.1.refs_7_), channel_id=1, source_target_pairs={{0,8},{4,12},{8,0},{12,4},{1,9},{5,13},{9,1},{13,5},{2,10},{6,14},... | collective-permute-start | bytes 1769480 | tf_op jit(solution)/shard_map/ppermute | solution.py:531
  50.8 40.7 %collective-permute-start = (bf16[384,768]{1,0:T(8,128)(2,1)S(1)}, bf16[384,768]{1,0:T(8,128)(2,1)}, u32[]{:S(2)}, u32[]{:S(2)}) collective-permute-start(bf16[384,768]{1,0:T(8,128)(2,1)S(1)} %copy-done), channel_id=1, source_target_pairs={{0,1},{1,2},{2,3},{4,5},{5,6},{6,7},{8,9},{9,10},{10,11},{12,13},{... | collective-permute-start | bytes 1769480 | tf_op jit(solution)/shard_map/ppermute | solution.py:603
  60.4 31.8 %collective-permute-start.9 = (bf16[4,192,384]{2,1,0:T(8,128)(2,1)S(1)}, bf16[4,192,384]{2,1,0:T(8,128)(2,1)S(1)}, u32[]{:S(2)}, u32[]{:S(2)}) collective-permute-start(bf16[4,192,384]{2,1,0:T(8,128)(2,1)S(1)} %pad_maximum_fusion.1.refs_7_), channel_id=1, source_target_pairs={{0,16},{16,0},{1,17},{17,1},{2,18},{18,2},{3,19},{19,3},{4,20},{20... | collective-permute-start | bytes 1769480 | tf_op jit(solution)/shard_map/ppermute | solution.py:540
  92.2 20.3 %collective-permute-start.1 = (bf16[384,768]{1,0:T(8,128)(2,1)}, bf16[384,768]{1,0:T(8,128)(2,1)}, u32[]{:S(2)}, u32[]{:S(2)}) collective-permute-start(bf16[384,768]{1,0:T(8,128)(2,1)} %collective-permute-done.refs_2_), channel_id=1, source_target_pairs={{0,1},{1,2},{2,3},{4,5},{5,6},{6,7},{8,9},{9,10},{10,11},{12,13},{... | collective-permute-start | bytes 1769480 | tf_op jit(solution)/shard_map/ppermute | solution.py:603
  112.6 37.0 %collective-permute-start.21 = (bf16[4,192,768]{2,1,0:T(8,128)(2,1)S(1)}, bf16[4,192,768]{2,1,0:T(8,128)(2,1)}, u32[]{:S(2)}, u32[]{:S(2)}) collective-permute-start(bf16[4,192,768]{2,1,0:T(8,128)(2,1)S(1)} %pad_maximum_fusion.refs_6_), channel_id=1, source_target_pairs={{0,16},{16,0},{1,17},{17,1},{2,18},{18,2},{3,19},{19,3},{4,20},{20... | collective-permute-start | bytes 3538952 | tf_op jit(solution)/shard_map/ppermute | solution.py:540
  112.6 21.3 %collective-permute-start.19 = (bf16[2,192,768]{2,1,0:T(8,128)(2,1)S(1)}, bf16[2,192,768]{2,1,0:T(8,128)(2,1)}, u32[]{:S(2)}, u32[]{:S(2)}) collective-permute-start(bf16[2,192,768]{2,1,0:T(8,128)(2,1)S(1)} %slice.160), channel_id=1, source_target_pairs={{0,8},{4,12},{8,0},{12,4},{1,9},{5,13},{9,1},{13,5},{2,10},{6,14},... | collective-permute-start | bytes 1769480 | tf_op jit(solution)/shard_map/ppermute | solution.py:534
  113.1 20.9 %collective-permute-start.20 = (bf16[2,192,768]{2,1,0:T(8,128)(2,1)S(1)}, bf16[2,192,768]{2,1,0:T(8,128)(2,1)}, u32[]{:S(2)}, u32[]{:S(2)}) collective-permute-start(bf16[2,192,768]{2,1,0:T(8,128)(2,1)S(1)} %slice.161), channel_id=1, source_target_pairs={{0,4},{4,0},{8,12},{12,8},{1,5},{5,1},{9,13},{13,9},{2,6},{6,2},{1... | collective-permute-start | bytes 1769480 | tf_op jit(solution)/shard_map/ppermute | solution.py:535
  114.6 34.9 %collective-permute-start.22 = (bf16[4,192,768]{2,1,0:T(8,128)(2,1)S(1)}, bf16[4,192,768]{2,1,0:T(8,128)(2,1)}, u32[]{:S(2)}, u32[]{:S(2)}) collective-permute-start(bf16[4,192,768]{2,1,0:T(8,128)(2,1)S(1)} %collective-permute-done.17.refs_7_), channel_id=1, source_target_pairs={{0,16},{16,0},{1,17},{17,1},{2,18},{18,2},{3,19},{19,3},{4,20},{20... | collective-permute-start | bytes 3538952 | tf_op jit(solution)/shard_map/ppermute | solution.py:540
  114.7 34.9 %collective-permute-start.23 = (bf16[4,192,768]{2,1,0:T(8,128)(2,1)}, bf16[4,192,768]{2,1,0:T(8,128)(2,1)}, u32[]{:S(2)}, u32[]{:S(2)}) collective-permute-start(bf16[4,192,768]{2,1,0:T(8,128)(2,1)} %collective-permute-done.18.refs_8_), channel_id=1, source_target_pairs={{0,16},{16,0},{1,17},{17,1},{2,18},{18,2},{3,19},{19,3},{4,20},{20... | collective-permute-start | bytes 3538952 | tf_op jit(solution)/shard_map/ppermute | solution.py:540
  185.4 154.0 %reduce-scatter.5.cloned.1.call-start = ((), (), s32[]{:S(2)}) async-start(), calls=%async_computation.2 | async-start | bytes 1474560 | tf_op jit(solution)/shard_map/reduce_scatter | solution.py:633
  229.2 18.3 %collective-permute-start.26 = (bf16[384,768]{1,0:T(8,128)(2,1)S(1)}, bf16[384,768]{1,0:T(8,128)(2,1)S(1)}, u32[]{:S(2)}, u32[]{:S(2)}) collective-permute-start(bf16[384,768]{1,0:T(8,128)(2,1)S(1)} %slice.225), channel_id=1, source_target_pairs={{1,0},{2,1},{3,2},{5,4},{6,5},{7,6},{9,8},{10,9},{11,10},{13,12},{... | collective-permute-start | bytes 1769480 | tf_op jit(solution)/shard_map/ppermute | solution.py:645
  238.0 15.7 %collective-permute-start.29 = (bf16[2,2,192,384]{3,2,1,0:T(8,128)(2,1)}, bf16[2,2,192,384]{3,2,1,0:T(8,128)(2,1)}, u32[]{:S(2)}, u32[]{:S(2)}) collective-permute-start(bf16[2,2,192,384]{3,2,1,0:T(8,128)(2,1)} %pad_maximum_fusion.2), channel_id=1, source_target_pairs={{0,4},{4,0},{8,12},{12,8},{1,5},{5,1},{9,13},{13,9},{2,6},{6,2},{1... | collective-permute-start | bytes 1769480 | tf_op jit(solution)/shard_map/ppermute | solution.py:553
  248.4 33.5 %collective-permute-start.27 = (bf16[384,768]{1,0:T(8,128)(2,1)}, bf16[384,768]{1,0:T(8,128)(2,1)S(1)}, u32[]{:S(2)}, u32[]{:S(2)}) collective-permute-start(bf16[384,768]{1,0:T(8,128)(2,1)} %add_convert_fusion.1), channel_id=1, source_target_pairs={{1,0},{2,1},{3,2},{5,4},{6,5},{7,6},{9,8},{10,9},{11,10},{13,12},{... | collective-permute-start | bytes 1769480 | tf_op jit(solution)/shard_map/ppermute | solution.py:645
  255.9 27.8 %collective-permute-start.30 = (bf16[2,192,384]{2,1,0:T(8,128)(2,1)}, bf16[2,192,384]{2,1,0:T(8,128)(2,1)}, u32[]{:S(2)}, u32[]{:S(2)}) collective-permute-start(bf16[2,192,384]{2,1,0:T(8,128)(2,1)} %get-tuple-element.87), channel_id=1, source_target_pairs={{0,8},{4,12},{8,0},{12,4},{1,9},{5,13},{9,1},{13,5},{2,10},{6,14},... | collective-permute-start | bytes 884744 | tf_op jit(solution)/shard_map/ppermute | solution.py:559
  257.5 26.2 %collective-permute-start.33 = (bf16[2,192,384]{2,1,0:T(8,128)(2,1)}, bf16[2,192,384]{2,1,0:T(8,128)(2,1)}, u32[]{:S(2)}, u32[]{:S(2)}) collective-permute-start(bf16[2,192,384]{2,1,0:T(8,128)(2,1)} %get-tuple-element.88), channel_id=1, source_target_pairs={{0,4},{4,0},{8,12},{12,8},{1,5},{5,1},{9,13},{13,9},{2,6},{6,2},{1... | collective-permute-start | bytes 884744 | tf_op jit(solution)/shard_map/ppermute | solution.py:560
  296.3 44.2 %collective-permute-start.36 = (f32[192,384]{1,0:T(8,128)S(1)}, f32[192,384]{1,0:T(8,128)S(1)}, u32[]{:S(2)}, u32[]{:S(2)}) collective-permute-start(f32[192,384]{1,0:T(8,128)S(1)} %fusion.12), channel_id=1, source_target_pairs={{0,16},{16,0},{1,17},{17,1},{2,18},{18,2},{3,19},{19,3},{4,20},{20... | collective-permute-start | bytes 884744 | tf_op jit(solution)/shard_map/ppermute | solution.py:657
  (44 other events, 532.9 us)
Sparse Core Ops, SparseCore 0:
  185.5 56.2 reduce-scatter.6
  250.0 36.0 reduce-scatter.4

commit v3 on v2

--- a/solution.py
+++ b/solution.py
@@ -334,45 +334,90 @@
     )(info, h, middle, dy, gain, w_out_t, *pieces)
 
 
-def mlp_grads_kernel(layout, info, keep_ref, got_ref, h_ref, h2_ref, dy_ref, dy2_ref, g_ref):
+def grad_slots(layout):
+    n_row, n_col = layout.n_row, layout.n_col
+    if n_row != 4:
+        return {(a, k): (0, (a, k)) for a in range(n_row) for k in range(n_col)}
+    cut = n_col // 2
+    slots = {}
+    for k in range(n_col):
+        slots[0, k] = (0, (k,))
+        if k < cut:
+            slots[1, k], slots[3, k], slots[2, k] = (1, (0, k)), (1, (1, k)), (3, (k,))
+        else:
+            slots[2, k], slots[3, k] = (2, (0, k - cut)), (2, (1, k - cut))
+            slots[1, k] = (4, (k - cut,))
+    return slots
+
+
+def grad_shapes(layout, deep, lanes):
+    n_row, n_col = layout.n_row, layout.n_col
+    if n_row != 4:
+        lead = [(n_row, n_col)]
+    else:
+        cut = n_col // 2
+        lead = [(n_col,), (2, cut), (2, n_col - cut), (cut,), (n_col - cut,)]
+    return tuple(jax.ShapeDtypeStruct(first + (deep, lanes), LOW) for first in lead)
+
+
+def row_of(layout, info, a, deep):
+    row = jnp.bitwise_xor(jnp.int32(a), layout.flip(info))
+    return pl.ds(pl.multiple_of(row * deep, 16), deep)
+
+
+def mlp_grads_kernel(layout, info, keep_ref, got_ref, h_ref, h2_ref, dy_ref, dy2_ref, *refs):
+    outs, (h_t, dy_t) = refs[:-2], refs[-2:]
     width = keep_ref.shape[1] // 3
     half = width // layout.n_col
-    deep = g_ref.shape[2]
-    h_t = jnp.concatenate([h_ref[...], h2_ref[...]], axis=0).T
-    dy_t = jnp.concatenate([dy_ref[...], dy2_ref[...]], axis=0).T
-    for step in range(layout.n_col):
-        col = lax.rem(layout.col(info) + (layout.n_col - step), layout.n_col)
+    deep = outs[0].shape[-2]
+    rows = h_ref.shape[0]
+    h_t[:, :rows] = h_ref[...].T
+    h_t[:, rows:] = h2_ref[...].T
+    dy_t[:, :rows] = dy_ref[...].T
+    dy_t[:, rows:] = dy2_ref[...].T
+    slots = grad_slots(layout)
+    for k in range(layout.n_col):
         for j, left in enumerate((dy_t, h_t, h_t)):
-            lanes = slice(j * width + step * half, j * width + (step + 1) * half)
+            lanes = slice(j * width + k * half, j * width + (k + 1) * half)
             right = jnp.concatenate([keep_ref[:, lanes], got_ref[:, lanes]], axis=0)
-            grad = contract(left, right, 1, 0).astype(LOW)
-            for row in range(layout.n_row):
-                g_ref[row, col, :, j * half : (j + 1) * half] = grad[
-                    row * deep : (row + 1) * deep
-                ]
-
-
-def mlp_grads(layout, info, keep, got, h, h_other, dy, dy_other):
+            for a in range(layout.n_row):
+                out, index = slots[a, k]
+                outs[out][(*index, slice(None), slice(j * half, (j + 1) * half))] = contract(
+                    left[row_of(layout, info, a, deep)], right, 1, 0
+                ).astype(LOW)
+
+
+def mlp_grads(layout, info, keep, got, h, h_other, dy, dy_other, *deps):
     rows, width = h.shape
     half = keep.shape[1] // 3 // layout.n_col
     vmem = pl.BlockSpec(memory_space=pltpu.VMEM)
-    shape = (layout.n_row, layout.n_col, width // layout.n_row, 3 * half)
+    shapes = grad_shapes(layout, width // layout.n_row, 3 * half)
     return pl.pallas_call(
-        functools.partial(mlp_grads_kernel, layout),
-        out_shape=jax.ShapeDtypeStruct(shape, LOW),
-        in_specs=[pl.BlockSpec(memory_space=pltpu.SMEM)] + [vmem] * 6,
-        out_specs=vmem,
+        with_deps(functools.partial(mlp_grads_kernel, layout), 7, len(deps)),
+        out_shape=shapes,
+        in_specs=[pl.BlockSpec(memory_space=pltpu.SMEM)]
+        + [vmem] * 6
+        + [pl.BlockSpec(memory_space=pl.ANY)] * len(deps),
+        out_specs=(vmem,) * len(shapes),
+        scratch_shapes=[pltpu.VMEM((width, 2 * rows), LOW)] * 2,
         compiler_params=pltpu.CompilerParams(vmem_limit_bytes=VMEM_LIMIT),
         cost_estimate=pl.CostEstimate(
             flops=4 * rows * width * keep.shape[1], bytes_accessed=12_000_000, transcendentals=0
         ),
         name="mlp_grads",
-    )(info, keep, got, h, h_other, dy, dy_other)
+    )(info, keep, got, h, h_other, dy, dy_other, *deps)
+
+
+def with_deps(kernel, count, deps):
+    def run(*refs):
+        kernel(*refs[:count], *refs[count + deps :])
+
+    return run
 
 
 def attend_backward_kernel(
     layout, info, q_ref, k_ref, v_ref, g_ref, cos_ref, sin_ref, cosq_ref, sinq_ref,
-    wq_ref, wk_ref, wv_ref, dq_ref, dk_ref, dv_ref, dseen_ref, dk_acc, dv_acc, dq_acc,
+    dq_ref, dk_ref, dv_ref, dk_acc, dv_acc,
 ):
     step = pl.program_id(0)
     steps = pl.num_programs(0)
@@ -392,7 +437,8 @@
         dv_acc[...] = jnp.zeros_like(dv_acc)
 
     cosine, sine = cosq_ref[...], -sinq_ref[...]
-    for pair in range(q_ref.shape[1] // PAIR):
+    pairs = q_ref.shape[1] // PAIR
+    for pair in range(pairs):
         lanes = slice(pair * PAIR, (pair + 1) * PAIR)
         query = split_heads(q_ref[:, lanes] * SCALE)
         grad = split_heads(g_ref[:, lanes])
@@ -406,110 +452,169 @@
         dv_acc[pl.ds(first, window), lanes] += contract(probs.astype(LOW), grad, 1, 0)
         dk_acc[pl.ds(first, window), lanes] += contract(grad_raw, query, 1, 0)
         grad_query = join_heads(contract(grad_raw, keys, 0, 0)) * SCALE
-        dq = rotate_pair(grad_query, cosine, sine).astype(LOW)
-        dq_ref[:, lanes] = dq
-        dq_acc[pl.ds(first, Q_ROWS), lanes] = dq
+        dq_ref[:, lanes] = rotate_pair(grad_query, cosine, sine).astype(LOW)
 
     @pl.when(step == steps - 1)
     def _():
-        rows = dq_acc.shape[0]
-        blocks = dk_acc.shape[0] // rows
-        for j in range(blocks):
-            place = slice(j * rows, (j + 1) * rows)
-            for pair in range(q_ref.shape[1] // PAIR):
-                lanes = slice(pair * PAIR, (pair + 1) * PAIR)
-                dk_ref[place, lanes] = rotate_pair(
-                    dk_acc[place, lanes], cos_ref[place], -sin_ref[place]
-                ).astype(LOW)
-                dv_ref[place, lanes] = dv_acc[place, lanes].astype(LOW)
-            seen = contract(dk_ref[place], wk_ref[...], 1, 1)
-            seen = seen + contract(dv_ref[place], wv_ref[...], 1, 1)
-            if j == blocks - 1:
-                seen = seen + contract(dq_acc[...], wq_ref[...], 1, 1)
-            dseen_ref[place] = seen
-
-
-def attend_backward(layout, info, query, keys, values, grads, cosine, sine, w_q, w_k, w_v):
+        for pair in range(pairs):
+            lanes = slice(pair * PAIR, (pair + 1) * PAIR)
+            dk_ref[:, lanes] = rotate_pair(dk_acc[:, lanes], cos_ref[...], -sin_ref[...]).astype(
+                LOW
+            )
+            dv_ref[:, lanes] = dv_acc[:, lanes].astype(LOW)
+
+
+def attend_backward(layout, info, part, parts, query, keys, values, grads, cosine, sine, *deps):
     rows, width = query.shape
     halo_steps = (keys.shape[0] - rows) // Q_ROWS
+    lanes = width // parts
+
+    def cols(array):
+        return pl.BlockSpec((array.shape[0], lanes), lambda i: (0, part))
 
     def whole(array):
         return pl.BlockSpec(array.shape, lambda i: (0, 0))
 
-    part = pl.BlockSpec((Q_ROWS, width), lambda i: (i, 0))
+    block = pl.BlockSpec((Q_ROWS, lanes), lambda i: (i, part))
     own = pl.BlockSpec((Q_ROWS, PAIR), lambda i: (halo_steps + i, 0))
+    flat = pl.BlockSpec((keys.shape[0], lanes), lambda i: (0, 0))
     return pl.pallas_call(
-        functools.partial(attend_backward_kernel, layout),
+        with_deps(functools.partial(attend_backward_kernel, layout), 9, len(deps)),
         out_shape=(
-            jax.ShapeDtypeStruct(query.shape, LOW),
-            jax.ShapeDtypeStruct(keys.shape, LOW),
-            jax.ShapeDtypeStruct(keys.shape, LOW),
-            jax.ShapeDtypeStruct(keys.shape, F32),
+            jax.ShapeDtypeStruct((rows, lanes), LOW),
+            jax.ShapeDtypeStruct((keys.shape[0], lanes), LOW),
+            jax.ShapeDtypeStruct((keys.shape[0], lanes), LOW),
         ),
         grid=(rows // Q_ROWS,),
         in_specs=[
-            pl.BlockSpec(memory_space=pltpu.SMEM), part, whole(keys), whole(values), part,
-            whole(cosine), whole(sine), own, own, whole(w_q), whole(w_k), whole(w_v),
-        ],
-        out_specs=(part, whole(keys), whole(keys), whole(keys)),
+            pl.BlockSpec(memory_space=pltpu.SMEM), block, cols(keys), cols(values), block,
+            whole(cosine), whole(sine), own, own,
+        ]
+        + [pl.BlockSpec(memory_space=pl.ANY)] * len(deps),
+        out_specs=(pl.BlockSpec((Q_ROWS, lanes), lambda i: (i, 0)), flat, flat),
         scratch_shapes=[
-            pltpu.VMEM(keys.shape, F32),
-            pltpu.VMEM(keys.shape, F32),
-            pltpu.VMEM(query.shape, LOW),
+            pltpu.VMEM((keys.shape[0], lanes), F32),
+            pltpu.VMEM((keys.shape[0], lanes), F32),
         ],
         compiler_params=pltpu.CompilerParams(vmem_limit_bytes=VMEM_LIMIT),
         cost_estimate=pl.CostEstimate(
-            flops=25_000_000_000, bytes_accessed=20_000_000, transcendentals=4_000_000
+            flops=25_000_000_000 // parts, bytes_accessed=20_000_000 // parts,
+            transcendentals=4_000_000 // parts,
         ),
         name="attend_backward",
-    )(info, query, keys, values, grads, cosine, sine, cosine, sine, w_q, w_k, w_v)
-
-
-def attend_grads_kernel(
-    layout, info, h_ref, dq_ref, dk_ref, dv_ref, heads_ref, dm_ref, keep_ref, send_ref
-):
-    rows = dq_ref.shape[0]
-    halo = h_ref.shape[0] - rows
-    deep = keep_ref.shape[2]
-    wide = keep_ref.shape[3] // 2
-    h_t = h_ref[...].T
-    dm_t = dm_ref[...].T
-    grads = (
-        contract(h_t[:, halo:], dq_ref[...], 1, 0).astype(LOW),
-        contract(h_t, dk_ref[...], 1, 0).astype(LOW),
-        contract(h_t, dv_ref[...], 1, 0).astype(LOW),
-        contract(dm_t, heads_ref[...], 1, 0).astype(LOW),
-    )
-    for core, (kept, sent) in enumerate(((keep_ref, send_ref), (send_ref, keep_ref))):
-
-        @pl.when(layout.core(info) == core)
-        def _(kept=kept, sent=sent):
-            for j, ref in enumerate((kept, kept, sent, sent)):
-                for row in range(layout.n_row):
-                    place = jnp.bitwise_xor(jnp.int32(row), layout.flip(info))
-                    for col in range(layout.n_col):
-                        step = lax.rem(layout.col(info) + (layout.n_col - col), layout.n_col)
-                        part = j % 2
-                        ref[place, step, :, part * wide : (part + 1) * wide] = grads[j][
-                            row * deep : (row + 1) * deep, col * wide : (col + 1) * wide
-                        ]
-
-
-def attend_grads(layout, info, h, dq, dk, dv, heads, dm):
-    rows, width = dq.shape
+    )(info, query, keys, values, grads, cosine, sine, cosine, sine, *deps)
+
+
+def seen_grads_kernel(parts, *refs):
+    seen = refs[: -(4 + 3 * parts + 4)]
+    wq_ref, wk_ref, wv_ref, gain_ref = refs[len(seen) : len(seen) + 4]
+    dqs = refs[len(seen) + 4 : len(seen) + 4 + parts]
+    dks = refs[len(seen) + 4 + parts : len(seen) + 4 + 2 * parts]
+    dvs = refs[len(seen) + 4 + 2 * parts : len(seen) + 4 + 3 * parts]
+    far_ref, near_ref, own_ref, dgain_ref = refs[-4:]
+    rows = seen[0].shape[0]
+    total = None
+    for j, tokens in enumerate(seen):
+        place = slice(j * rows, (j + 1) * rows)
+        dk = jnp.concatenate([ref[place] for ref in dks], axis=1)
+        dv = jnp.concatenate([ref[place] for ref in dvs], axis=1)
+        grad = contract(dk, wk_ref[...], 1, 1) + contract(dv, wv_ref[...], 1, 1)
+        if j == len(seen) - 1:
+            dq = jnp.concatenate([ref[...] for ref in dqs], axis=1)
+            grad = grad + contract(dq, wq_ref[...], 1, 1)
+            own_ref[...] = grad
+        elif j == 0:
+            far_ref[...] = grad.astype(LOW)
+        else:
+            near_ref[(j - 1) * rows : j * rows] = grad
+        x = tokens[...].astype(F32)
+        scale = lax.rsqrt(jnp.mean(x * x, axis=1, keepdims=True) + EPSILON)
+        gained = jnp.sum(grad * x * scale, axis=0, keepdims=True)
+        total = gained if total is None else total + gained
+    dgain_ref[...] = total
+
+
+def seen_grads(seen, w_q, w_k, w_v, gain, dqs, dks, dvs):
+    rows, width = seen[0].shape
     vmem = pl.BlockSpec(memory_space=pltpu.VMEM)
-    shape = (layout.n_row, layout.n_col, width // layout.n_row, 2 * width // layout.n_col)
+    parts = len(dqs)
+    args = (*seen, w_q, w_k, w_v, gain, *dqs, *dks, *dvs)
     return pl.pallas_call(
-        functools.partial(attend_grads_kernel, layout),
-        out_shape=(jax.ShapeDtypeStruct(shape, LOW),) * 2,
-        in_specs=[pl.BlockSpec(memory_space=pltpu.SMEM)] + [vmem] * 6,
-        out_specs=(vmem, vmem),
+        functools.partial(seen_grads_kernel, parts),
+        out_shape=(
+            jax.ShapeDtypeStruct((rows, width), LOW),
+            jax.ShapeDtypeStruct((rows * (len(seen) - 2), width), F32),
+            jax.ShapeDtypeStruct((rows, width), F32),
+            jax.ShapeDtypeStruct((1, width), F32),
+        ),
+        in_specs=[vmem] * len(args),
+        out_specs=(vmem,) * 4,
+        compiler_params=pltpu.CompilerParams(vmem_limit_bytes=VMEM_LIMIT),
+        cost_estimate=pl.CostEstimate(
+            flops=14 * rows * width * width, bytes_accessed=12_000_000, transcendentals=0
+        ),
+        name="seen_grads",
+    )(*args)
+
+
+def attend_grads_kernel(layout, parts, *refs):
+    info = refs[0]
+    longs, shorts = refs[1:3], refs[3:5]
+    keep_long, got_long = refs[5 : 5 + parts], refs[5 + parts : 5 + 2 * parts]
+    keep_short, got_short = refs[5 + 2 * parts : 7 + 2 * parts]
+    outs, (long_t, short_t) = refs[7 + 2 * parts : -2], refs[-2:]
+    deep = outs[0].shape[-2]
+    wide = outs[0].shape[-1] // 2
+    seen, rows = longs[0].shape[0], shorts[0].shape[0]
+    for j in range(2):
+        long_t[:, j * seen : (j + 1) * seen] = longs[j][...].T
+        short_t[:, j * rows : (j + 1) * rows] = shorts[j][...].T
+    slots = grad_slots(layout)
+    right_short = jnp.concatenate([keep_short[...], got_short[...]], axis=0)
+    right_long = jnp.concatenate(
+        [
+            jnp.concatenate([ref[...] for ref in keep_long], axis=1),
+            jnp.concatenate([ref[...] for ref in got_long], axis=1),
+        ],
+        axis=0,
+    )
+    for a in range(layout.n_row):
+        place = row_of(layout, info, a, deep)
+        for j, (left, right) in enumerate(((short_t, right_short), (long_t, right_long))):
+            grad = contract(left[place], right, 1, 0).astype(LOW)
+            for col in range(layout.n_col):
+                block = grad[:, col * wide : (col + 1) * wide]
+                step = lax.rem(layout.col(info) + (layout.n_col - col), layout.n_col)
+                for k in range(layout.n_col):
+                    out, index = slots[a, k]
+
+                    @pl.when(step == k)
+                    def _(out=out, index=index, block=block, j=j):
+                        outs[out][
+                            (*index, slice(None), slice(j * wide, (j + 1) * wide))
+                        ] = block
+
+
+def attend_grads(layout, info, longs, shorts, keep_long, got_long, keep_short, got_short):
+    rows, width = shorts[0].shape
+    vmem = pl.BlockSpec(memory_space=pltpu.VMEM)
+    shapes = grad_shapes(layout, width // layout.n_row, 2 * width // layout.n_col)
+    args = (*longs, *shorts, *keep_long, *got_long, keep_short, got_short)
+    return pl.pallas_call(
+        functools.partial(attend_grads_kernel, layout, len(keep_long)),
+        out_shape=shapes,
+        in_specs=[pl.BlockSpec(memory_space=pltpu.SMEM)] + [vmem] * len(args),
+        out_specs=(vmem,) * len(shapes),
+        scratch_shapes=[
+            pltpu.VMEM((width, 2 * longs[0].shape[0]), LOW),
+            pltpu.VMEM((width, 2 * rows), LOW),
+        ],
         compiler_params=pltpu.CompilerParams(vmem_limit_bytes=VMEM_LIMIT),
         cost_estimate=pl.CostEstimate(
             flops=16 * rows * width * width, bytes_accessed=12_000_000, transcendentals=0
         ),
         name="attend_grads",
-    )(info, h, dq, dk, dv, heads, dm)
+    )(info, *args)
 
 
 def shift(count, by):
@@ -519,24 +624,31 @@
 SWAP = [(0, 1), (1, 0)]
 
 
-def gather(layout, block):
-    n_row, n_col = layout.n_row, layout.n_col
-    plane = jnp.stack(
-        [block] + [lax.ppermute(block, "col", shift(n_col, k)) for k in range(1, n_col)]
-    )
-    if n_row == 4:
+def after(value, *deps):
+    return lax.optimization_barrier((value, *deps))[0]
+
+
+def gather_cols(layout, block):
+    n_col = layout.n_col
+    return [block] + [lax.ppermute(block, "col", shift(n_col, k)) for k in range(1, n_col)]
+
+
+def gather_rows(layout, plane):
+    if layout.n_row == 4:
         along_x = [(i, i ^ 1) for i in range(4)]
         along_y = [(i, i ^ 2) for i in range(4)]
         from_x = lax.ppermute(plane, "row", along_x)
         from_y = lax.ppermute(plane, "row", along_y)
-        cut = n_col // 2
+        cut = layout.n_col // 2
         diagonal = (
             lax.ppermute(from_x[:cut], "row", along_y),
             lax.ppermute(from_y[cut:], "row", along_x),
         )
-        pieces = [plane, from_x, from_y, *diagonal]
-    else:
-        pieces = [lax.all_gather(plane, "row", axis=0, tiled=True)]
+        return [plane, from_x, from_y, *diagonal]
+    return [lax.all_gather(plane, "row", axis=0, tiled=True)]
+
+
+def both_cores(pieces):
     return pieces + [lax.ppermute(piece, "ba", SWAP) for piece in pieces]
 
 
@@ -544,32 +656,63 @@
     return left.astype(F32) + right.astype(F32)
 
 
-def scatter(layout, grads):
-    n_row, n_col = layout.n_row, layout.n_col
-    if n_row == 4:
-        along_x = [(i, i ^ 1) for i in range(4)]
-        along_y = [(i, i ^ 2) for i in range(4)]
-        cut = n_col // 2
-        got_x = lax.ppermute(
-            jnp.stack([grads[1, :cut], grads[3, :cut]]), "row", along_x
-        )
-        got_y = lax.ppermute(
-            jnp.stack([grads[2, cut:], grads[3, cut:]]), "row", along_y
-        )
-        on_y = lax.ppermute(plus(grads[2, :cut], got_x[1]).astype(LOW), "row", along_y)
-        on_x = lax.ppermute(plus(grads[1, cut:], got_y[1]).astype(LOW), "row", along_x)
-        plane = jnp.concatenate(
-            [
-                plus(grads[0, :cut], got_x[0]) + on_y.astype(F32),
-                plus(grads[0, cut:], got_y[0]) + on_x.astype(F32),
-            ]
-        ).astype(LOW)
-    else:
-        plane = lax.psum_scatter(grads, "row", scatter_dimension=0, tiled=True)[0]
-    total = plane[0].astype(F32)
-    for k in range(1, n_col):
-        total = total + lax.ppermute(plane[k], "col", shift(n_col, n_col - k)).astype(F32)
+def scatter_start(layout, grads):
+    if layout.n_row != 4:
+        return (lax.psum_scatter(grads[0], "row", scatter_dimension=0, tiled=True)[0],)
+    _, for_x, for_y, _, _ = grads
+    return (
+        lax.ppermute(for_x, "row", [(i, i ^ 1) for i in range(4)]),
+        lax.ppermute(for_y, "row", [(i, i ^ 2) for i in range(4)]),
+    )
+
+
+def scatter_next(layout, grads, got):
+    if layout.n_row != 4:
+        return got
+    got_x, got_y = got
+    _, _, _, on_y, on_x = grads
+    return (
+        plus(on_y, got_x[1]).astype(LOW),
+        plus(on_x, got_y[1]).astype(LOW),
+    )
+
+
+def scatter_plane(layout, grads, got, sums):
+    if layout.n_row != 4:
+        return got[0]
+    from_y = lax.ppermute(sums[0], "row", [(i, i ^ 2) for i in range(4)])
+    from_x = lax.ppermute(sums[1], "row", [(i, i ^ 1) for i in range(4)])
+    cut = layout.n_col // 2
+    own = grads[0]
+    return [
+        (plus(own[k], got[0][0, k]) + from_y[k].astype(F32)).astype(LOW)
+        if k < cut
+        else (plus(own[k], got[1][0, k - cut]) + from_x[k - cut].astype(F32)).astype(LOW)
+        for k in range(layout.n_col)
+    ]
+
+
+def scatter_cols(layout, plane):
+    n_col = layout.n_col
+    return [plane[0]] + [
+        lax.ppermute(plane[k], "col", shift(n_col, n_col - k)) for k in range(1, n_col)
+    ]
+
+
+def add_up(blocks):
+    total = blocks[0].astype(F32)
+    for block in blocks[1:]:
+        total = total + block.astype(F32)
     return total
+
+
+def sum_everywhere(values, sizes):
+    for axis, size in sizes:
+        by = 1
+        while by < size:
+            values = values + lax.ppermute(values, axis, [(i, i ^ by) for i in range(size)])
+            by *= 2
+    return values
 
 
 def shards(
@@ -597,11 +740,17 @@
         jnp.concatenate([w_gate, w_down_t[:, :half_units]], axis=1),
         jnp.concatenate([w_up, w_down_t[:, half_units:]], axis=1),
     )
-    attn_pieces = gather(layout, attn_block)
+    attn_cols = gather_cols(layout, attn_block)
+    mlp_cols = gather_cols(layout, after(mlp_block, *attn_cols))
+    attn_plane = jnp.stack(attn_cols)
+    attn_pieces = gather_rows(layout, attn_plane)
     blocks = [tokens]
-    for _ in range(hops):
-        blocks.insert(0, lax.ppermute(blocks[0], "col", step_right))
-    mlp_pieces = gather(layout, mlp_block)
+    for hop in range(hops):
+        sent = after(blocks[0], *mlp_cols) if hop == 0 else blocks[0]
+        blocks.insert(0, lax.ppermute(sent, "col", step_right))
+    mlp_plane = after(jnp.stack(mlp_cols), *attn_pieces)
+    attn_pieces = both_cores(attn_pieces)
+    mlp_pieces = both_cores(gather_rows(layout, mlp_plane))
     dy_other = lax.ppermute(cotangent, "ba", SWAP)
 
     first = col * rows
@@ -623,42 +772,66 @@
     heads, middle, h2 = attend_forward(
         layout, info, q, k, v, w_o_t, tokens, gain_mlp[None]
     )
+    h1_other = lax.ppermute(h1, "ba", SWAP)
     h2_other = lax.ppermute(h2, "ba", SWAP)
     layer_out, keep, send, d_middle, dm, d_heads, dgain_mlp = mlp(
         layout, info, h2, middle, cotangent, gain_mlp[None], w_o_t, mlp_pieces
     )
     got = lax.ppermute(send, "ba", SWAP)
-    grads_mlp = mlp_grads(layout, info, keep, got, h2, h2_other, cotangent, dy_other)
-    part = lax.psum_scatter(grads_mlp, "row", scatter_dimension=0, tiled=True)
-    part = lax.psum_scatter(part, "col", scatter_dimension=1, tiled=True)[0, 0]
-
-    dq, dk, dv, d_seen = attend_backward(
-        layout, info, q, k, v, d_heads, cosine, sine, w_q, w_k, w_v
-    )
-    keep_attn, send_attn = attend_grads(layout, info, h1, dq, dk, dv, heads, dm)
-    got_attn = lax.ppermute(send_attn, "ba", SWAP)
-    part_attn = scatter(layout, plus(keep_attn, got_attn).astype(LOW))
-
-    d_h1 = d_seen[halo:]
-    travelling = d_seen[:rows].astype(LOW)
+    short = jnp.where(first_core, h1[halo:], dm)
+    short_other = lax.ppermute(jnp.where(first_core, dm, h1[halo:]), "ba", SWAP)
+
+    def backward(part, *deps):
+        return attend_backward(
+            layout, info, part, 3, q, k, v, d_heads, cosine, sine, *deps
+        )
+
+    grads = [backward(0)]
+    grads_mlp = mlp_grads(
+        layout, info, keep, got, h2, h2_other, cotangent, dy_other, grads[0][0]
+    )
+    got_mlp = scatter_start(layout, grads_mlp)
+    grads.append(backward(1, grads_mlp[0]))
+    sums_mlp = scatter_next(layout, grads_mlp, after(got_mlp, grads[1][0]))
+    grads.append(backward(2, *sums_mlp))
+    plane_mlp = scatter_plane(layout, grads_mlp, got_mlp, sums_mlp)
+    dqs, dks, dvs = zip(*grads)
+    keep_long = [jnp.where(first_core, dk, dv) for dk, dv in zip(dks, dvs)]
+    send_long = [jnp.where(first_core, dv, dk) for dk, dv in zip(dks, dvs)]
+    got_long = [lax.ppermute(value, "ba", SWAP) for value in send_long]
+    dq = jnp.concatenate(dqs, axis=1)
+    keep_short = jnp.where(first_core, dq, heads)
+    got_short = lax.ppermute(jnp.where(first_core, heads, dq), "ba", SWAP)
+    far, near, own, dgain_attn = seen_grads(
+        blocks, w_q, w_k, w_v, gain_attn[None], dqs, dks, dvs
+    )
+    grads_attn = attend_grads(
+        layout, info, (h1, h1_other), (short, short_other), keep_long, got_long,
+        keep_short, got_short,
+    )
+    got_attn = scatter_start(layout, grads_attn)
+    d_h1 = own
+    travelling = far
     for hop in range(hops):
         arrived = lax.ppermute(travelling, "col", step_left).astype(F32)
         if hop + 1 < hops:
-            travelling = (d_seen[(hop + 1) * rows : (hop + 2) * rows] + arrived).astype(LOW)
+            travelling = (near[hop * rows : (hop + 1) * rows] + arrived).astype(LOW)
         else:
             d_h1 = d_h1 + arrived
+    part = add_up(scatter_cols(layout, plane_mlp))
+    sums_attn = scatter_next(layout, grads_attn, got_attn)
+    plane_attn = scatter_plane(layout, grads_attn, got_attn, sums_attn)
+    part_attn = add_up(scatter_cols(layout, plane_attn))
     x = tokens.astype(F32)
     scale = lax.rsqrt(jnp.mean(x * x, axis=1, keepdims=True) + EPSILON)
     weighted = d_h1 * gain_attn[None, :]
     inner = jnp.mean(weighted * x, axis=1, keepdims=True)
     input_grad = (d_middle + scale * weighted - x * (scale**3 * inner)).astype(LOW)
-    dgain_attn = jnp.sum(d_h1 * x * scale, axis=0)
 
     other_attn = lax.ppermute(part_attn, "ba", SWAP)
-    lower = jnp.where(first_core, part_attn, other_attn)
-    upper = jnp.where(first_core, other_attn, part_attn)
+    zero_side = jnp.where(first_core, part_attn, other_attn)
+    one_side = jnp.where(first_core, other_attn, part_attn)
     wide = width // n_col
-    part = part.astype(F32)
     other = lax.ppermute(part, "ba", SWAP)
     cut = part.shape[1] // 3
 
@@ -668,10 +841,13 @@
             [jnp.where(first_core, mine, theirs), jnp.where(first_core, theirs, mine)], axis=1
         )
 
-    grad_gain_attn, grad_gain_mlp = lax.psum((dgain_attn, dgain_mlp[0]), ("ba", "row", "col"))
+    gains = sum_everywhere(
+        jnp.concatenate([dgain_attn, dgain_mlp]),
+        (("ba", 2), ("row", n_row), ("col", n_col)),
+    )
     return (
-        layer_out, input_grad, lower[:, :wide], lower[:, wide:], upper[:, :wide],
-        upper[:, wide:].T, whole(1), whole(2), whole(0).T, grad_gain_attn, grad_gain_mlp,
+        layer_out, input_grad, zero_side[:, :wide], zero_side[:, wide:], one_side[:, wide:],
+        one_side[:, :wide].T, whole(1), whole(2), whole(0).T, gains[0], gains[1],
     )
 
 

time: 356 us -> 327 us (0.919)
  blocking collectives: 40.5 us -> 0 us
  Pallas kernels: 99 us -> 114 us
  between operations: 17.4 us -> 4.2 us
  starting transfers between devices: 61.2 us -> 73.7 us
    psum x1 -> x0, blocking collectives: 40.5 us -> none  [shards(): lax.psum((dgain_attn, dgain_mlp[0]), ('ba', 'row', 'col'))]
    ppermute x34 -> x51, waiting for transfers between devices: 63.2 us -> 90.5 us  [the longest x6 28.7 us: scatter_cols(): lax.ppermute(plane[k], 'col', shift(n_col, n_col - k))]
    ppermute x2, waiting for transfers between devices: 29.7 us -> 6.58 us  [shards(): arrived = lax.ppermute(travelling, 'col', step_left).astype(F32)]
    pallas_call x3 -> x6, Pallas kernels: 52.6 us -> 67.9 us  [the longest x3 35.5 us: attend_backward(): pl.pallas_call(with_deps(functools.partial(attend_backward_kernel, layout...]
    ppermute x34 -> x51, starting transfers between devices: 57.6 us -> 69.8 us  [the longest x2 13.6 us: shards(): blocks.insert(0, lax.ppermute(sent, 'col', step_right))]
    select_n x1 -> x6, other arithmetic: 0.04 us -> 5.8 us  [the longest x3 3.96 us: shards(): send_long = [jnp.where(first_core, dv, dk) for dk, dv in zip(dks, dvs)]]
    ppermute x1, waiting for transfers between devices: 4.48 us -> 0.01 us  [shards(): dy_other = lax.ppermute(cotangent, 'ba', SWAP)]
  transfers between devices with their start and end apart: 43 -> 58, of which waited for: 16 -> 17; matrix products, arithmetic and copies ran while one was open for 8% -> 8% of each run, Pallas kernels for 20% -> 30%
where the time goes in v3:
time: 327 us; the launch traced here: 324 us
  Pallas kernels  114 us (35%)
  waiting for transfers between devices  97.1 us (30%)
  starting transfers between devices  73.7 us (23%)
  other arithmetic  20.8 us (6%)
  local copies, waits for them, and re-layouts  14.1 us (4%)
  between operations  4.2 us (1%)
    pallas_call x3, Pallas kernels, attend_backward(): pl.pallas_call(with_deps(functools.partial(attend_backward_kernel, layout...  35.5 us
    ppermute x6, waiting for transfers between devices, scatter_cols(): lax.ppermute(plane[k], 'col', shift(n_col, n_col - k))  28.7 us
    pallas_call x1, Pallas kernels, mlp(): pl.pallas_call(functools.partial(mlp_kernel, layout), out_shape=(like((ro...  17.8 us
    pallas_call x1, Pallas kernels, attend_grads(): pl.pallas_call(functools.partial(attend_grads_kernel, layout, len(keep_lo...  15.3 us
    ppermute x2, waiting for transfers between devices, shards(): blocks.insert(0, lax.ppermute(sent, 'col', step_right))  15 us
    pallas_call x1, Pallas kernels, attend_forward(): pl.pallas_call(functools.partial(attend_forward_kernel, layout), out_shap...  15 us
    ppermute x2, starting transfers between devices, shards(): blocks.insert(0, lax.ppermute(sent, 'col', step_right))  13.6 us
    ppermute x5, waiting for transfers between devices, sum_everywhere(): lax.ppermute(values, axis, [(i, i ^ by) for i in range(size)])  13.6 us
  transfers between devices with their start and end apart: 58, of which 17 were waited for; matrix products, arithmetic and copies ran while one was open for 8% of the time, Pallas kernels for 30%

profile of v3, /device:TPU:0, one launch (start us, length us, event | category | flops | bytes accessed | tf_op | source)
XLA Modules:
  0.0 324.1 jit_solution(10984300101349622814)
XLA Ops:
  12.7 5.5 %collective-permute-done.1 = bf16[192,384]{1,0:T(8,128)(2,1)S(1)} collective-permute-done((bf16[192,384]{1,0:T(8,128)(2,1)S(1)}, bf16[192,384]{1,0:T(8,128)(2,1)S(1)}, u32[]{:S(2)}, u32[]{:S(2)}) %collective-permute-start.1) | collective-permute-done | bytes 147488 | tf_op jit(solution)/shard_map/ppermute | solution.py:633
  21.5 3.7 %collective-permute-start.3 = (bf16[192,768]{1,0:T(8,128)(2,1)S(1)}, bf16[192,768]{1,0:T(8,128)(2,1)S(1)}, u32[]{:S(2)}, u32[]{:S(2)}) collective-permute-start(bf16[192,768]{1,0:T(8,128)(2,1)S(1)} %maximum_select_fusion), channel_id=1, source_target_pairs={{0,1},{1,2},{2,3},{3,0},{4,5},{5,6},{6,7},{7,4},{8,9},{9,10},{10,1... | collective-permute-start | bytes 884744 | tf_op jit(solution)/shard_map/ppermute | solution.py:633
  27.6 6.0 %collective-permute-done.8.refs_8_ = bf16[4,192,384]{2,1,0:T(8,128)(2,1)} collective-permute-done((bf16[4,192,384]{2,1,0:T(8,128)(2,1)S(1)}, bf16[4,192,384]{2,1,0:T(8,128)(2,1)}, u32[]{:S(2)}, u32[]{:S(2)}) %collective-permute-start.8) | collective-permute-done | bytes 589856 | tf_op jit(solution)/shard_map/ppermute | solution.py:640
  38.8 5.8 %collective-permute-done.4 = bf16[192,768]{1,0:T(8,128)(2,1)S(1)} collective-permute-done((bf16[192,768]{1,0:T(8,128)(2,1)S(1)}, bf16[192,768]{1,0:T(8,128)(2,1)S(1)}, u32[]{:S(2)}, u32[]{:S(2)}) %collective-permute-start.4) | collective-permute-done | bytes 294944 | tf_op jit(solution)/shard_map/ppermute | solution.py:633
  47.1 8.3 %collective-permute-start.6 = (bf16[384,768]{1,0:T(8,128)(2,1)S(1)}, bf16[384,768]{1,0:T(8,128)(2,1)}, u32[]{:S(2)}, u32[]{:S(2)}) collective-permute-start(bf16[384,768]{1,0:T(8,128)(2,1)S(1)} %copy-done.1), channel_id=1, source_target_pairs={{0,1},{1,2},{2,3},{4,5},{5,6},{6,7},{8,9},{9,10},{10,11},{12,13},{... | collective-permute-start | bytes 1769480 | tf_op jit(solution)/shard_map/ppermute | solution.py:750
  55.9 11.9 %collective-permute-done.6.refs_2_.refs_1_ = bf16[384,768]{1,0:T(8,128)(2,1)} collective-permute-done((bf16[384,768]{1,0:T(8,128)(2,1)S(1)}, bf16[384,768]{1,0:T(8,128)(2,1)}, u32[]{:S(2)}, u32[]{:S(2)}) %collective-permute-start.6) | collective-permute-done | bytes 589856 | tf_op jit(solution)/shard_map/ppermute | solution.py:750
  67.9 5.3 %collective-permute-start.7 = (bf16[384,768]{1,0:T(8,128)(2,1)}, bf16[384,768]{1,0:T(8,128)(2,1)}, u32[]{:S(2)}, u32[]{:S(2)}) collective-permute-start(bf16[384,768]{1,0:T(8,128)(2,1)} %collective-permute-done.6.refs_2_.refs_1_), channel_id=1, source_target_pairs={{0,1},{1,2},{2,3},{4,5},{5,6},{6,7},{8,9},{9,10},{10,11},{12,13},{... | collective-permute-start | bytes 1769480 | tf_op jit(solution)/shard_map/ppermute | solution.py:750
  85.1 3.8 %fusion.6 = (f32[1152,128]{1,0:T(8,128)}, f32[1152,128]{1,0:T(8,128)}) fusion(f32[128]{0:T(128)S(1)} %get-tuple-element.156, f32[128]{0:T(128)S(1)} %get-tuple-element.157, f32[1152]{0:T(1024)S(1)} %subtract_convert_fusion), kind=kLoop, calls=%fused_computation.16 | loop fusion | flops 294912 | bytes 1185280 | tf_op jit(solution)/shard_map/mul | solution.py:767
  90.6 13.6 %project.1 = (bf16[1152,768]{1,0:T(8,128)(2,1)}, bf16[384,768]{1,0:T(8,128)(2,1)}, bf16[1152,768]{1,0:T(8,128)(2,1)}, bf16[1152,768]{1,0:T(8,128)(2,1)}, bf16[76...) custom-call(s32[8]{0:T(128)} %concatenate.56.refs_0_.info, ...), custom_call_target="tpu_custom_call" | custom-call | flops 4076863488 | bytes 20000000 | tf_op jit(solution)/shard_map/project/pallas_call | solution.py:151
  104.9 15.0 %attend_forward.1 = (bf16[384,768]{1,0:T(8,128)(2,1)}, f32[384,768]{1,0:T(8,128)}, bf16[384,768]{1,0:T(8,128)(2,1)}) custom-call(s32[8]{0:T(128)} %concatenate.56.refs_0_.info, bf16[384,768]{1,0:T(8,128)(2,1)} %get-tuple-element.59.q_ref.refs_1_, bf16[1152,768]{1,0:T(8,128)(2,1)} %get-tuple-element.60.k_ref.refs_2_, ...), custom_call_target="tpu_custom_call" | custom-call | flops 8000000000 | bytes 9000000 | tf_op jit(solution)/shard_map/attend_forward/pallas_call | solution.py:207
  120.9 17.8 %mlp.1 = (bf16[384,768]{1,0:T(8,128)(2,1)}, bf16[384,3072]{1,0:T(8,128)(2,1)}, bf16[384,3072]{1,0:T(8,128)(2,1)}, f32[384,768]{1,0:T(8,128)}, bf16[384,768]{1,0:...) custom-call(s32[8]{0:T(128)} %concatenate.56.refs_0_.info, ...), custom_call_target="tpu_custom_call" | custom-call | flops 7247757312 | bytes 20000000 | tf_op jit(solution)/shard_map/mlp/pallas_call | solution.py:308
  139.9 11.8 %attend_backward.3 = (bf16[384,256]{1,0:T(8,128)(2,1)}, bf16[1152,256]{1,0:T(8,128)(2,1)}, bf16[1152,256]{1,0:T(8,128)(2,1)}) custom-call(s32[8]{0:T(128)} %concatenate.56.refs_0_.info, bf16[384,768]{1,0:T(8,128)(2,1)} %get-tuple-element.59.q_ref.refs_1_, bf16[1152,768]{1,0:T(8,128)(2,1)} %get-tuple-element.60.k_ref.refs_2_, ...), custom_call_target="tpu_custom_call" | custom-call | flops 8333333504 | bytes 6666666 | tf_op jit(solution)/shard_map/attend_backward/pallas_call | solution.py:481
  156.0 8.8 %mlp_grads.1 = (bf16[4,192,768]{2,1,0:T(8,128)(2,1)}, bf16[2,2,192,768]{3,2,1,0:T(8,128)(2,1)}, bf16[2,2,192,768]{3,2,1,0:T(8,128)(2,1)}, bf16[2,192,768]{2,1,0:T(8,128)(2,1)}, bf16[2,192,768]{2,1,0:T(8,128)(2,1)}) custom-call(s32[8]{0:T(128)} %concatenate.56.refs_0_.info, bf16[384,3072]{1,0:T(8,128)(2,1)} %get-tuple-element.73.refs_1_, ...), custom_call_target="tpu_custom_call" | custom-call | flops 3623878656 | bytes 12000000 | tf_op jit(solution)/shard_map/mlp_grads/pallas_call | solution.py:395
  168.7 11.7 %attend_backward.4 = (bf16[384,256]{1,0:T(8,128)(2,1)}, bf16[1152,256]{1,0:T(8,128)(2,1)}, bf16[1152,256]{1,0:T(8,128)(2,1)}) custom-call(s32[8]{0:T(128)} %concatenate.56.refs_0_.info, bf16[384,768]{1,0:T(8,128)(2,1)} %get-tuple-element.59.q_ref.refs_1_, bf16[1152,768]{1,0:T(8,128)(2,1)} %get-tuple-element.60.k_ref.refs_2_, ...), custom_call_target="tpu_custom_call" | custom-call | flops 8333333504 | bytes 6666666 | tf_op jit(solution)/shard_map/attend_backward/pallas_call | solution.py:481
  180.5 12.5 %collective-permute-done.29 = bf16[2,2,192,768]{3,2,1,0:T(8,128)(2,1)S(1)} collective-permute-done((bf16[2,2,192,768]{3,2,1,0:T(8,128)(2,1)}, bf16[2,2,192,768]{3,2,1,0:T(8,128)(2,1)S(1)}, u32[]{:S(2)}, u32[]{:S(2)}) %collective-permute-start.29) | collective-permute-done | bytes 1179680 | tf_op jit(solution)/shard_map/ppermute | solution.py:664
  196.2 12.0 %attend_backward.5 = (bf16[384,256]{1,0:T(8,128)(2,1)}, bf16[1152,256]{1,0:T(8,128)(2,1)}, bf16[1152,256]{1,0:T(8,128)(2,1)}) custom-call(s32[8]{0:T(128)} %concatenate.56.refs_0_.info, bf16[384,768]{1,0:T(8,128)(2,1)} %get-tuple-element.59.q_ref.refs_1_, bf16[1152,768]{1,0:T(8,128)(2,1)} %get-tuple-element.60.k_ref.refs_2_, ...), custom_call_target="tpu_custom_call" | custom-call | flops 8333333504 | bytes 6666666 | tf_op jit(solution)/shard_map/attend_backward/pallas_call | solution.py:481
  208.2 8.4 %seen_grads.1 = (bf16[384,768]{1,0:T(8,128)(2,1)}, f32[384,768]{1,0:T(8,128)}, f32[384,768]{1,0:T(8,128)}, f32[1,768]{1,0:T(1,128)}) custom-call(bf16[384,768]{1,0:T(8,128)(2,1)} %collective-permute-done.7.refs_1_.refs_0_, bf16[384,768]{1,0:T(8,128)(2,1)} %collective-permute-done.6.refs_2_.refs_1_, bf16[384,768]{1,0:T(8,128)(2,1)} %refs_2_.1, ...), custom_call_target="tpu_custom_call" | custom-call | flops 3170893824 | bytes 12000000 | tf_op jit(solution)/shard_map/seen_grads/pallas_call | solution.py:542
  224.9 11.0 %collective-permute-done.55 = f32[2,768]{1,0:T(2,128)S(1)} collective-permute-done((f32[2,768]{1,0:T(2,128)S(1)}, f32[2,768]{1,0:T(2,128)S(1)}, u32[]{:S(2)}, u32[]{:S(2)}) %collective-permute-start.55) | collective-permute-done | bytes 6176 | tf_op jit(solution)/shard_map/ppermute | solution.py:713
  246.7 4.5 %collective-permute-start.48 = (bf16[192,768]{1,0:T(8,128)(2,1)S(1)}, bf16[192,768]{1,0:T(8,128)(2,1)S(1)}, u32[]{:S(2)}, u32[]{:S(2)}) collective-permute-start(bf16[192,768]{1,0:T(8,128)(2,1)S(1)} %get-tuple-element.130), channel_id=1, source_target_pairs={{0,3},{1,0},{2,1},{3,2},{4,7},{5,4},{6,5},{7,6},{8,11},{9,8},{10,9... | collective-permute-start | bytes 884744 | tf_op jit(solution)/shard_map/ppermute | solution.py:698
  253.7 15.3 %attend_grads.1 = (bf16[4,192,384]{2,1,0:T(8,128)(2,1)}, bf16[2,2,192,384]{3,2,1,0:T(8,128)(2,1)}, bf16[2,2,192,384]{3,2,1,0:T(8,128)(2,1)}, bf16[2,192,384]{2,1,0:T(8,128)(2,1)}, bf16[2,192,384]{2,1,0:T(8,128)(2,1)}) custom-call(s32[8]{0:T(128)} %concatenate.56.refs_0_.info, bf16[1152,768]{1,0:T(8,128)(2,1)} %get-tuple-element.93.refs_1_, ...), custom_call_target="tpu_custom_call" | custom-call | flops 3623878656 | bytes 12000000 | tf_op jit(solution)/shard_map/attend_grads/pallas_call | solution.py:603
  273.7 16.4 %collective-permute-done.50 = bf16[192,768]{1,0:T(8,128)(2,1)S(1)} collective-permute-done((bf16[192,768]{1,0:T(8,128)(2,1)S(1)}, bf16[192,768]{1,0:T(8,128)(2,1)S(1)}, u32[]{:S(2)}, u32[]{:S(2)}) %collective-permute-start.50) | collective-permute-done | bytes 294944 | tf_op jit(solution)/shard_map/ppermute | solution.py:698
  293.2 6.6 %collective-permute-done.32 = bf16[384,768]{1,0:T(8,128)(2,1)S(1)} collective-permute-done((bf16[384,768]{1,0:T(8,128)(2,1)S(1)}, bf16[384,768]{1,0:T(8,128)(2,1)S(1)}, u32[]{:S(2)}, u32[]{:S(2)}) %collective-permute-start.32) | collective-permute-done | bytes 589856 | tf_op jit(solution)/shard_map/ppermute | solution.py:816
  302.5 4.0 %collective-permute-start.44 = (bf16[192,384]{1,0:T(8,128)(2,1)S(1)}, bf16[192,384]{1,0:T(8,128)(2,1)S(1)}, u32[]{:S(2)}, u32[]{:S(2)}) collective-permute-start(bf16[192,384]{1,0:T(8,128)(2,1)S(1)} %get-tuple-element.122), channel_id=1, source_target_pairs={{0,2},{1,3},{2,0},{3,1},{4,6},{5,7},{6,4},{7,5},{8,10},{9,11},{10,... | collective-permute-start | bytes 442376 | tf_op jit(solution)/shard_map/ppermute | solution.py:698
  308.2 10.7 %collective-permute-done.44 = bf16[192,384]{1,0:T(8,128)(2,1)S(1)} collective-permute-done((bf16[192,384]{1,0:T(8,128)(2,1)S(1)}, bf16[192,384]{1,0:T(8,128)(2,1)S(1)}, u32[]{:S(2)}, u32[]{:S(2)}) %collective-permute-start.44) | collective-permute-done | bytes 147488 | tf_op jit(solution)/shard_map/ppermute | solution.py:698
  (248 shorter events, 89.7 us)
Async XLA Ops:
  25.2 19.4 %collective-permute-start.4 = (bf16[192,768]{1,0:T(8,128)(2,1)S(1)}, bf16[192,768]{1,0:T(8,128)(2,1)S(1)}, u32[]{:S(2)}, u32[]{:S(2)}) collective-permute-start(bf16[192,768]{1,0:T(8,128)(2,1)S(1)} %maximum_select_fusion), channel_id=1, source_target_pairs={{0,2},{1,3},{2,0},{3,1},{4,6},{5,7},{6,4},{7,5},{8,10},{9,11},{10,... | collective-permute-start | bytes 884744 | tf_op jit(solution)/shard_map/ppermute | solution.py:633
  45.1 28.1 %collective-permute-start.17 = (bf16[4,192,768]{2,1,0:T(8,128)(2,1)S(1)}, bf16[4,192,768]{2,1,0:T(8,128)(2,1)S(1)}, u32[]{:S(2)}, u32[]{:S(2)}) collective-permute-start(bf16[4,192,768]{2,1,0:T(8,128)(2,1)S(1)} %pad_maximum_fusion.refs_6_), channel_id=1, source_target_pairs={{0,4},{4,0},{8,12},{12,8},{1,5},{5,1},{9,13},{13,9},{2,6},{6,2},{1... | collective-permute-start | bytes 3538952 | tf_op jit(solution)/shard_map/ppermute | solution.py:640
  46.6 26.6 %collective-permute-start.18 = (bf16[4,192,768]{2,1,0:T(8,128)(2,1)S(1)}, bf16[4,192,768]{2,1,0:T(8,128)(2,1)}, u32[]{:S(2)}, u32[]{:S(2)}) collective-permute-start(bf16[4,192,768]{2,1,0:T(8,128)(2,1)S(1)} %pad_maximum_fusion.refs_6_), channel_id=1, source_target_pairs={{0,8},{4,12},{8,0},{12,4},{1,9},{5,13},{9,1},{13,5},{2,10},{6,14},... | collective-permute-start | bytes 3538952 | tf_op jit(solution)/shard_map/ppermute | solution.py:641
  47.1 20.7 %collective-permute-start.6 = (bf16[384,768]{1,0:T(8,128)(2,1)S(1)}, bf16[384,768]{1,0:T(8,128)(2,1)}, u32[]{:S(2)}, u32[]{:S(2)}) collective-permute-start(bf16[384,768]{1,0:T(8,128)(2,1)S(1)} %copy-done.1), channel_id=1, source_target_pairs={{0,1},{1,2},{2,3},{4,5},{5,6},{6,7},{8,9},{9,10},{10,11},{12,13},{... | collective-permute-start | bytes 1769480 | tf_op jit(solution)/shard_map/ppermute | solution.py:750
  55.4 23.3 %collective-permute-start.13 = (bf16[4,192,384]{2,1,0:T(8,128)(2,1)}, bf16[4,192,384]{2,1,0:T(8,128)(2,1)}, u32[]{:S(2)}, u32[]{:S(2)}) collective-permute-start(bf16[4,192,384]{2,1,0:T(8,128)(2,1)} %collective-permute-done.8.refs_8_), channel_id=1, source_target_pairs={{0,16},{16,0},{1,17},{17,1},{2,18},{18,2},{3,19},{19,3},{4,20},{20... | collective-permute-start | bytes 1769480 | tf_op jit(solution)/shard_map/ppermute | solution.py:652
  55.6 23.3 %collective-permute-start.14 = (bf16[4,192,384]{2,1,0:T(8,128)(2,1)}, bf16[4,192,384]{2,1,0:T(8,128)(2,1)}, u32[]{:S(2)}, u32[]{:S(2)}) collective-permute-start(bf16[4,192,384]{2,1,0:T(8,128)(2,1)} %collective-permute-done.9.refs_9_), channel_id=1, source_target_pairs={{0,16},{16,0},{1,17},{17,1},{2,18},{18,2},{3,19},{19,3},{4,20},{20... | collective-permute-start | bytes 1769480 | tf_op jit(solution)/shard_map/ppermute | solution.py:652
  78.8 41.1 %collective-permute-start.21 = (bf16[4,192,768]{2,1,0:T(8,128)(2,1)S(1)}, bf16[4,192,768]{2,1,0:T(8,128)(2,1)}, u32[]{:S(2)}, u32[]{:S(2)}) collective-permute-start(bf16[4,192,768]{2,1,0:T(8,128)(2,1)S(1)} %pad_maximum_fusion.refs_6_), channel_id=1, source_target_pairs={{0,16},{16,0},{1,17},{17,1},{2,18},{18,2},{3,19},{19,3},{4,20},{20... | collective-permute-start | bytes 3538952 | tf_op jit(solution)/shard_map/ppermute | solution.py:652
  78.9 25.3 %collective-permute-start.19 = (bf16[2,192,768]{2,1,0:T(8,128)(2,1)S(1)}, bf16[2,192,768]{2,1,0:T(8,128)(2,1)}, u32[]{:S(2)}, u32[]{:S(2)}) collective-permute-start(bf16[2,192,768]{2,1,0:T(8,128)(2,1)S(1)} %slice.209), channel_id=1, source_target_pairs={{0,8},{4,12},{8,0},{12,4},{1,9},{5,13},{9,1},{13,5},{2,10},{6,14},... | collective-permute-start | bytes 1769480 | tf_op jit(solution)/shard_map/ppermute | solution.py:644
  80.5 24.3 %collective-permute-start.20 = (bf16[2,192,768]{2,1,0:T(8,128)(2,1)S(1)}, bf16[2,192,768]{2,1,0:T(8,128)(2,1)}, u32[]{:S(2)}, u32[]{:S(2)}) collective-permute-start(bf16[2,192,768]{2,1,0:T(8,128)(2,1)S(1)} %slice.210), channel_id=1, source_target_pairs={{0,4},{4,0},{8,12},{12,8},{1,5},{5,1},{9,13},{13,9},{2,6},{6,2},{1... | collective-permute-start | bytes 1769480 | tf_op jit(solution)/shard_map/ppermute | solution.py:645
  82.0 37.9 %collective-permute-start.22 = (bf16[4,192,768]{2,1,0:T(8,128)(2,1)S(1)}, bf16[4,192,768]{2,1,0:T(8,128)(2,1)}, u32[]{:S(2)}, u32[]{:S(2)}) collective-permute-start(bf16[4,192,768]{2,1,0:T(8,128)(2,1)S(1)} %collective-permute-done.17.refs_7_), channel_id=1, source_target_pairs={{0,16},{16,0},{1,17},{17,1},{2,18},{18,2},{3,19},{19,3},{4,20},{20... | collective-permute-start | bytes 3538952 | tf_op jit(solution)/shard_map/ppermute | solution.py:652
  85.1 34.8 %collective-permute-start.23 = (bf16[4,192,768]{2,1,0:T(8,128)(2,1)}, bf16[4,192,768]{2,1,0:T(8,128)(2,1)}, u32[]{:S(2)}, u32[]{:S(2)}) collective-permute-start(bf16[4,192,768]{2,1,0:T(8,128)(2,1)} %collective-permute-done.18.refs_8_), channel_id=1, source_target_pairs={{0,16},{16,0},{1,17},{17,1},{2,18},{18,2},{3,19},{19,3},{4,20},{20... | collective-permute-start | bytes 3538952 | tf_op jit(solution)/shard_map/ppermute | solution.py:652
  139.8 103.4 %collective-permute-start.33 = (bf16[1152,768]{1,0:T(8,128)(2,1)S(1)}, bf16[1152,768]{1,0:T(8,128)(2,1)}, u32[]{:S(2)}, u32[]{:S(2)}) collective-permute-start(bf16[1152,768]{1,0:T(8,128)(2,1)S(1)} %copy-done.22), channel_id=1, source_target_pairs={{0,16},{16,0},{1,17},{17,1},{2,18},{18,2},{3,19},{19,3},{4,20},{20... | collective-permute-start | bytes 5308424 | tf_op jit(solution)/shard_map/ppermute | solution.py:775
  153.8 89.4 %collective-permute-start.35 = (bf16[1152,256]{1,0:T(8,128)(2,1)S(1)}, bf16[1152,256]{1,0:T(8,128)(2,1)S(1)}, u32[]{:S(2)}, u32[]{:S(2)}) collective-permute-start(bf16[1152,256]{1,0:T(8,128)(2,1)S(1)} %get-tuple-element.137), channel_id=1, source_target_pairs={{0,16},{16,0},{1,17},{17,1},{2,18},{18,2},{3,19},{19,3},{4,20},{20... | collective-permute-start | bytes 1769480 | tf_op jit(solution)/shard_map/ppermute | solution.py:801
  164.8 28.2 %collective-permute-start.29 = (bf16[2,2,192,768]{3,2,1,0:T(8,128)(2,1)}, bf16[2,2,192,768]{3,2,1,0:T(8,128)(2,1)S(1)}, u32[]{:S(2)}, u32[]{:S(2)}) collective-permute-start(bf16[2,2,192,768]{3,2,1,0:T(8,128)(2,1)} %get-tuple-element.78), channel_id=1, source_target_pairs={{0,4},{4,0},{8,12},{12,8},{1,5},{5,1},{9,13},{13,9},{2,6},{6,2},{1... | collective-permute-start | bytes 3538952 | tf_op jit(solution)/shard_map/ppermute | solution.py:664
  166.3 27.9 %collective-permute-start.30 = (bf16[2,2,192,768]{3,2,1,0:T(8,128)(2,1)}, bf16[2,2,192,768]{3,2,1,0:T(8,128)(2,1)S(1)}, u32[]{:S(2)}, u32[]{:S(2)}) collective-permute-start(bf16[2,2,192,768]{3,2,1,0:T(8,128)(2,1)} %get-tuple-element.79), channel_id=1, source_target_pairs={{0,8},{4,12},{8,0},{12,4},{1,9},{5,13},{9,1},{13,5},{2,10},{6,14},... | collective-permute-start | bytes 3538952 | tf_op jit(solution)/shard_map/ppermute | solution.py:665
  219.2 25.3 %collective-permute-start.49 = (bf16[2,192,768]{2,1,0:T(8,128)(2,1)S(1)}, bf16[2,192,768]{2,1,0:T(8,128)(2,1)S(1)}, u32[]{:S(2)}, u32[]{:S(2)}) collective-permute-start(bf16[2,192,768]{2,1,0:T(8,128)(2,1)S(1)} %copy-done.10), channel_id=1, source_target_pairs={{0,4},{4,0},{8,12},{12,8},{1,5},{5,1},{9,13},{13,9},{2,6},{6,2},{1... | collective-permute-start | bytes 1769480 | tf_op jit(solution)/shard_map/ppermute | solution.py:684
  220.8 24.2 %collective-permute-start.47 = (bf16[2,192,768]{2,1,0:T(8,128)(2,1)S(1)}, bf16[2,192,768]{2,1,0:T(8,128)(2,1)S(1)}, u32[]{:S(2)}, u32[]{:S(2)}) collective-permute-start(bf16[2,192,768]{2,1,0:T(8,128)(2,1)S(1)} %copy-done.9), channel_id=1, source_target_pairs={{0,8},{4,12},{8,0},{12,4},{1,9},{5,13},{9,1},{13,5},{2,10},{6,14},... | collective-permute-start | bytes 1769480 | tf_op jit(solution)/shard_map/ppermute | solution.py:683
  245.0 25.6 %collective-permute-start.31 = (bf16[384,768]{1,0:T(8,128)(2,1)}, bf16[384,768]{1,0:T(8,128)(2,1)S(1)}, u32[]{:S(2)}, u32[]{:S(2)}) collective-permute-start(bf16[384,768]{1,0:T(8,128)(2,1)} %get-tuple-element.92), channel_id=1, source_target_pairs={{1,0},{2,1},{3,2},{5,4},{6,5},{7,6},{9,8},{10,9},{11,10},{13,12},{... | collective-permute-start | bytes 1769480 | tf_op jit(solution)/shard_map/ppermute | solution.py:816
  246.7 25.5 %collective-permute-start.48 = (bf16[192,768]{1,0:T(8,128)(2,1)S(1)}, bf16[192,768]{1,0:T(8,128)(2,1)S(1)}, u32[]{:S(2)}, u32[]{:S(2)}) collective-permute-start(bf16[192,768]{1,0:T(8,128)(2,1)S(1)} %get-tuple-element.130), channel_id=1, source_target_pairs={{0,3},{1,0},{2,1},{3,2},{4,7},{5,4},{6,5},{7,6},{8,11},{9,8},{10,9... | collective-permute-start | bytes 884744 | tf_op jit(solution)/shard_map/ppermute | solution.py:698
  251.2 38.9 %collective-permute-start.50 = (bf16[192,768]{1,0:T(8,128)(2,1)S(1)}, bf16[192,768]{1,0:T(8,128)(2,1)S(1)}, u32[]{:S(2)}, u32[]{:S(2)}) collective-permute-start(bf16[192,768]{1,0:T(8,128)(2,1)S(1)} %get-tuple-element.118), channel_id=1, source_target_pairs={{0,2},{1,3},{2,0},{3,1},{4,6},{5,7},{6,4},{7,5},{8,10},{9,11},{10,... | collective-permute-start | bytes 884744 | tf_op jit(solution)/shard_map/ppermute | solution.py:698
  251.2 38.9 %collective-permute-start.51 = (bf16[192,768]{1,0:T(8,128)(2,1)S(1)}, bf16[192,768]{1,0:T(8,128)(2,1)S(1)}, u32[]{:S(2)}, u32[]{:S(2)}) collective-permute-start(bf16[192,768]{1,0:T(8,128)(2,1)S(1)} %get-tuple-element.119), channel_id=1, source_target_pairs={{0,1},{1,2},{2,3},{3,0},{4,5},{5,6},{6,7},{7,4},{8,9},{9,10},{10,1... | collective-permute-start | bytes 884744 | tf_op jit(solution)/shard_map/ppermute | solution.py:698
  269.0 21.4 %collective-permute-start.39 = (bf16[2,2,192,384]{3,2,1,0:T(8,128)(2,1)}, bf16[2,2,192,384]{3,2,1,0:T(8,128)(2,1)S(1)}, u32[]{:S(2)}, u32[]{:S(2)}) collective-permute-start(bf16[2,2,192,384]{3,2,1,0:T(8,128)(2,1)} %get-tuple-element.97), channel_id=1, source_target_pairs={{0,4},{4,0},{8,12},{12,8},{1,5},{5,1},{9,13},{13,9},{2,6},{6,2},{1... | collective-permute-start | bytes 1769480 | tf_op jit(solution)/shard_map/ppermute | solution.py:664
  270.6 21.5 %collective-permute-start.42 = (bf16[2,2,192,384]{3,2,1,0:T(8,128)(2,1)}, bf16[2,2,192,384]{3,2,1,0:T(8,128)(2,1)S(1)}, u32[]{:S(2)}, u32[]{:S(2)}) collective-permute-start(bf16[2,2,192,384]{3,2,1,0:T(8,128)(2,1)} %get-tuple-element.99), channel_id=1, source_target_pairs={{0,8},{4,12},{8,0},{12,4},{1,9},{5,13},{9,1},{13,5},{2,10},{6,14},... | collective-permute-start | bytes 1769480 | tf_op jit(solution)/shard_map/ppermute | solution.py:665
  272.2 27.6 %collective-permute-start.32 = (bf16[384,768]{1,0:T(8,128)(2,1)S(1)}, bf16[384,768]{1,0:T(8,128)(2,1)S(1)}, u32[]{:S(2)}, u32[]{:S(2)}) collective-permute-start(bf16[384,768]{1,0:T(8,128)(2,1)S(1)} %add_convert_fusion), channel_id=1, source_target_pairs={{1,0},{2,1},{3,2},{5,4},{6,5},{7,6},{9,8},{10,9},{11,10},{13,12},{... | collective-permute-start | bytes 1769480 | tf_op jit(solution)/shard_map/ppermute | solution.py:816
  (81 other events, 866.3 us)
